TPU v7x, 32 devices: a whole 2x2x4 slice. The times are simulated.
32 devices in a mesh: tile: 8 (over z, y), member: 4 (over x, core).
Axes of the slice: x: 2, y: 2, z: 4, core: 2. Of those that a mesh axis runs over, the one named last changes fastest.
Arguments:
- latent: float32 [4, 4, 64, 8192], P('member', None, None, 'tile'), may hold values from -6 to 6
- noise: float32 [4, 4, 64, 8192], P('member', None, None, 'tile'), may hold values from -6 to 6
- features: bfloat16 [64, 64, 8192], P('member', None, 'tile'), may hold values from -6 to 6
- slot_window: int32 [48], P('tile'), may hold values from -1 to 254, as said below
- timestep: int32 [1], replicated, may hold values from 200 to 999
- time_weight: bfloat16 [64, 64], replicated, may hold values from -0.75 to 0.75
- in_weight: bfloat16 [64, 36], replicated, may hold values from -1 to 1
- conv1_weight: bfloat16 [64, 576], replicated, may hold values from -0.25 to 0.25
- conv2_weight: bfloat16 [64, 576], replicated, may hold values from -0.25 to 0.25
- out_weight: bfloat16 [4, 576], replicated, may hold values from -0.25 to 0.25
- norm1_gain: float32 [64], replicated, may hold values from 0.1 to 1.9
- norm2_gain: float32 [64], replicated, may hold values from 0.1 to 1.9
- norm3_gain: float32 [64], replicated, may hold values from 0.1 to 1.9
Outputs:
- latent_prev: float32 [4, 4, 64, 8192], P('member', None, None, 'tile')
Inputs may be any that keep to these rules, and one draw needn't show every extreme that they name: `slot_window`: entry j of tile t's 6 slots (index t * 6 + j) is -1 for an empty slot or a window whose columns all lie in tiles t - 1 to t + 1; a window may be listed in several slots, and each listing counts.
All inputs are finite; a program needn't handle non-finite values.
Results may differ from a plain program's by a relative error of at most 0.0003.
Values may be sent and summed in bfloat16 or wider, within the bound.
A program may use at most 128 MiB of HBM per device.

v0:
```python
import math

import jax
import jax.numpy as jnp
from jax import lax
from jax.sharding import PartitionSpec as P

LAT = 4
WIN = 64
REACH = 1
TRAIN_STEPS = 1000
STRIDE = 20
GROUPS = 32


norm_epsilon = 1e-05
eta_noise = 0.5
beta_first = 0.00085
beta_last = 0.012


def with_halo(block, sides, width):
    for axis, dim in sides:
        count = lax.axis_size(axis)
        forward = [(i, i + 1) for i in range(count - 1)]
        backward = [(target, source) for source, target in forward]
        low = lax.ppermute(
            lax.slice_in_dim(block, block.shape[dim] - width, None, axis=dim), axis, forward
        )
        high = lax.ppermute(lax.slice_in_dim(block, 0, width, axis=dim), axis, backward)
        block = jnp.concatenate([low, block, high], axis=dim)
    return block


def from_behind(value, axis, by):
    length = lax.axis_size(axis)
    pairs = [(i, i + by) for i in range(length) if 0 <= i + by < length]
    return lax.ppermute(value, axis, pairs)


def plan_terms(timestep):
    betas_root = jnp.linspace(beta_first**0.5, beta_last**0.5, TRAIN_STEPS, dtype=jnp.float32)
    alpha_bar = jnp.cumprod(1.0 - betas_root * betas_root)
    current = alpha_bar[timestep[0]]
    earlier = alpha_bar[timestep[0] - STRIDE]
    sigma_sq = eta_noise * eta_noise * (1.0 - earlier) / (1.0 - current) * (1.0 - current / earlier)
    return (current, earlier, sigma_sq)


def time_embed(timestep, time_weight):
    half_width = time_weight.shape[0] // 2
    freqs_row = jnp.exp(-math.log(10000.0) * jnp.arange(half_width, dtype=jnp.float32) / half_width)
    angles = timestep[0].astype(jnp.float32) * freqs_row
    embedding = jnp.concatenate([jnp.cos(angles), jnp.sin(angles)]).astype(jnp.bfloat16)
    return jax.nn.silu(
        jnp.dot(embedding[None, :], time_weight, preferred_element_type=jnp.float32)[0]
    )


def conv_same(activation, weight, window_side):
    cell_count = activation.shape[-1]
    column = jnp.arange(cell_count, dtype=jnp.int32) % window_side
    padded = jnp.pad(activation, ((0, 0), (window_side + 1, window_side + 1)))
    tap_list = []
    for row_shift in (-1, 0, 1):
        for col_shift in (-1, 0, 1):
            anchor = window_side + 1 + row_shift * window_side + col_shift
            tap_piece = padded[:, anchor : anchor + cell_count]
            if col_shift == -1:
                tap_piece = jnp.where(column >= 1, tap_piece, jnp.zeros_like(tap_piece))
            if col_shift == 1:
                tap_piece = jnp.where(
                    column <= window_side - 2, tap_piece, jnp.zeros_like(tap_piece)
                )
            tap_list.append(tap_piece)
    stacked = jnp.concatenate(tap_list, axis=0)
    return jnp.dot(weight, stacked, preferred_element_type=jnp.float32)


def group_norm(hidden, gain):
    channels, cell_count = hidden.shape
    grouped = hidden.reshape(GROUPS, channels // GROUPS * cell_count)
    center = jnp.mean(grouped, axis=1, keepdims=True)
    deviate = grouped - center
    spread_sq = jnp.mean(deviate * deviate, axis=1, keepdims=True)
    normed = (deviate * lax.rsqrt(spread_sq + norm_epsilon)).reshape(channels, cell_count)
    return normed * gain[:, None]


def denoiser(latent_win, feature_win, time_bias, weight_set):
    in_weight, conv1_weight, conv2_weight, out_weight, gain_one, gain_two, gain_three = weight_set
    hidden = conv_same(latent_win, in_weight, WIN) + feature_win.astype(jnp.float32)
    first_act = jax.nn.silu(group_norm(hidden, gain_one)).astype(jnp.bfloat16)
    middle = conv_same(first_act, conv1_weight, WIN) + time_bias[:, None]
    second_act = jax.nn.silu(group_norm(middle, gain_two)).astype(jnp.bfloat16)
    block_out = hidden + conv_same(second_act, conv2_weight, WIN)
    third_act = jax.nn.silu(group_norm(block_out, gain_three)).astype(jnp.bfloat16)
    return conv_same(third_act, out_weight, WIN)


def denoise_update(state_now, eps_mean, noise_draw, current, earlier, sigma_sq):
    clean_est = (state_now - jnp.sqrt(1.0 - current) * eps_mean) / jnp.sqrt(current)
    return (
        jnp.sqrt(earlier) * clean_est
        + jnp.sqrt(1.0 - earlier - sigma_sq) * eps_mean
        + jnp.sqrt(sigma_sq) * noise_draw
    )


def body(
    latent,
    noise,
    features,
    slot_window,
    timestep,
    time_weight,
    in_weight,
    conv1_weight,
    conv2_weight,
    out_weight,
    norm1_gain,
    norm2_gain,
    norm3_gain,
):
    tile_width = latent.shape[-1]
    half_win = WIN // 2
    rim_width = REACH * tile_width
    ext_width = tile_width + 2 * rim_width
    tile_index = lax.axis_index("tile")
    all_channels = lax.all_gather(features, "member", axis=0, tiled=True)
    driver_ext = with_halo(all_channels, (("tile", 2),), rim_width)
    latent_ext = with_halo(latent[0].astype(jnp.bfloat16), (("tile", 2),), rim_width)
    current, earlier, sigma_sq = plan_terms(timestep)
    time_bias = time_embed(timestep, time_weight)
    weight_set = (
        in_weight,
        conv1_weight,
        conv2_weight,
        out_weight,
        norm1_gain,
        norm2_gain,
        norm3_gain,
    )
    listed = slot_window >= 0
    listed_weight = listed.astype(jnp.float32)
    local_start = jnp.where(
        listed, slot_window * half_win - tile_index * tile_width + rim_width, rim_width
    )
    channels = driver_ext.shape[0]

    def one_slot(start_col):
        latent_win = lax.dynamic_slice_in_dim(latent_ext, start_col, WIN, 2).reshape(LAT, WIN * WIN)
        feature_win = lax.dynamic_slice_in_dim(driver_ext, start_col, WIN, 2).reshape(
            channels, WIN * WIN
        )
        return denoiser(latent_win, feature_win, time_bias, weight_set)

    eps_slots = lax.map(one_slot, local_start)

    def add_slot(running, packed):
        start_col, eps_window, weight_one = packed
        current_slab = lax.dynamic_slice_in_dim(running, start_col, WIN, 2)
        updated = current_slab + weight_one * eps_window.reshape(LAT, WIN, WIN)
        return (lax.dynamic_update_slice_in_dim(running, updated, start_col, 2), None)

    partial_ext, ignored = lax.scan(
        add_slot,
        jnp.zeros((LAT, WIN, ext_width), jnp.float32),
        (local_start, eps_slots, listed_weight),
    )
    ext_cols = jnp.arange(ext_width, dtype=jnp.int32)
    inside = (ext_cols[None, :] >= local_start[:, None]) & (
        ext_cols[None, :] < local_start[:, None] + WIN
    )
    cover_ext = jnp.sum(listed_weight[:, None] * inside.astype(jnp.float32), axis=0)
    eps_total = partial_ext[:, :, rim_width : rim_width + tile_width]
    cover_total = cover_ext[rim_width : rim_width + tile_width]
    distance = 1
    low_col = rim_width + distance * tile_width
    sums_piece = partial_ext[:, :, low_col : low_col + tile_width]
    count_piece = cover_ext[low_col : low_col + tile_width]
    got_sums = from_behind(sums_piece.astype(jnp.bfloat16), "tile", distance).astype(
        sums_piece.dtype
    )
    got_count = from_behind(count_piece.astype(jnp.bfloat16), "tile", distance).astype(
        count_piece.dtype
    )
    eps_total = eps_total + got_sums
    cover_total = cover_total + got_count
    distance = 1
    high_col = rim_width - (distance - 1) * tile_width
    low_col = high_col - tile_width
    sums_piece = partial_ext[:, :, low_col:high_col]
    count_piece = cover_ext[low_col:high_col]
    got_sums = from_behind(sums_piece.astype(jnp.bfloat16), "tile", -distance).astype(
        sums_piece.dtype
    )
    got_count = from_behind(count_piece.astype(jnp.bfloat16), "tile", -distance).astype(
        count_piece.dtype
    )
    eps_total = eps_total + got_sums
    cover_total = cover_total + got_count
    eps_mean = eps_total / jnp.maximum(cover_total, 1.0)[None, None, :]
    return denoise_update(latent[0], eps_mean, noise[0], current, earlier, sigma_sq)[None]


def solution(mesh):
    placed = (
        P("member", None, None, "tile"),
        P("member", None, None, "tile"),
        P("member", None, "tile"),
        P("tile"),
        P(),
        P(),
        P(),
        P(),
        P(),
        P(),
        P(),
        P(),
        P(),
    )
    return jax.shard_map(
        body, mesh=mesh, in_specs=placed, out_specs=P("member", None, None, "tile"), check_vma=False
    )
```

profile of v0, /device:TPU:17, one launch (start us, length us, event | category | flops | bytes accessed | tf_op | source)
XLA Modules:
  0.0 683.7 jit_solution(995018977964579854)
XLA Ops:
  7.3 61.5 %all-gather.2.cloned.1.call-done = bf16[64,64,1024]{2,1,0:T(8,128)(2,1)} async-done(((bf16[16,64,1024]{2,1,0:T(8,128)(2,1)}), bf16[64,64,1024]{2,1,0:T(8,128)(2,1)}) %all-gather.2.cloned.1.call-update) | async-done | bytes 8388624 | tf_op jit(solution)/shard_map/all_gather | solution.py:130
  68.7 3.1 collective-permute-start.2
  71.8 3.1 collective-permute-start.3
  76.2 2.2 collective-permute-start
  78.4 4.0 collective-permute-start.1
  84.5 1.9 collective-permute-start.6
  87.8 366.1 %collective-permute-done = bf16[4,64,1024]{2,1,0:T(8,128)(2,1)S(1)} collective-permute-done((bf16[4,64,1024]{2,1,0:T(8,128)(2,1)S(1)}, bf16[4,64,1024]{2,1,0:T(8,128)(2,1)S(1)}, u32[]{:S(2)}, u32[]{:S(2)}) %collective-permute-start) | collective-permute-done | bytes 524320 | tf_op jit(solution)/shard_map/ppermute | solution.py:27
  453.9 4.1 collective-permute-start.7
  458.2 17.6 %pad_maximum_fusion = bf16[64,64,3072]{2,1,0:T(8,128)(2,1)} fusion(bf16[64,64,1024]{2,1,0:T(8,128)(2,1)} %collective-permute-done.3, bf16[64,64,1024]{2,1,0:T(8,128)(2,1)} %all-gather.2.cloned.1.call-done, bf16[64,64,1024]{2,1,0:T(8,128)(2,1)} %collective-permute-done.2), kind=kLoop, calls=%fused_computation.70 | loop fusion | flops 75497472 | bytes 50331648 | tf_op jit(solution)/shard_map/concatenate | solution.py:31
  475.8 127.3 %while.22 = (s32[]{:T(128)}, f32[6,4,4096]{2,1,0:T(4,128)}, s32[6]{0:T(128)S(1)}, bf16[4,64,3072]{2,1,0:T(8,128)(2,1)S(1)}, bf16[64,36]{0,1:T(8,128)(2,1)S(1)}, ...) while((s32[]{:T(128)}, f32[6,4,4096]{2,1,0:T(4,128)}, ...), condition=%wide.region_15.16_spmd, body=%wide.region_2.15_spmd.sunk | while | flops 663355456 | bytes 75635800 | solution.py:158
  479.0 1.6 dynamic-slice_convert_fusion.2
  499.9 2.0 dynamic-slice_convert_fusion.2
  521.2 2.0 dynamic-slice_convert_fusion.2
  542.4 2.0 dynamic-slice_convert_fusion.2
  563.7 2.0 dynamic-slice_convert_fusion.2
  585.0 2.0 dynamic-slice_convert_fusion.2
  603.4 40.7 %while.23 = (s32[]{:T(128)}, f32[4,64,3072]{2,1,0:T(8,128)S(1)}, s32[6]{0:T(128)S(1)}, f32[6]{0:T(128)}, f32[6,4,4096]{2,1,0:T(4,128)}, /*index=5*/s32[]{:T(128)}, s32[]{:T(128)}, s32[]{:T(128)}) while((s32[]{:T(128)}, f32[4,64,3072]{2,1,0:T(8,128)S(1)}, s32[6]{0:T(128)S(1)}, f32[6]{0:T(128)}, f32[6,4,4096]{2,1,0:T(4,128)}, ...), condition=%wide.region_17.18_spmd, body=%wide.region_16.17_spmd.sunk | while | flops 32773 | bytes 589983 | solution.py:166
  607.5 1.5 dynamic-slice_multiply_fusion.2
  614.4 1.5 dynamic-slice_multiply_fusion.2
  645.4 1.9 collective-permute-start.4
  647.3 4.2 collective-permute-start.5
  657.2 11.8 %collective-permute-done.4 = bf16[4,64,1024]{2,1,0:T(8,128)(2,1)} collective-permute-done((bf16[4,64,1024]{2,1,0:T(8,128)(2,1)}, bf16[4,64,1024]{2,1,0:T(8,128)(2,1)}, u32[]{:S(2)}, u32[]{:S(2)}) %collective-permute-start.4) | collective-permute-done | bytes 524320 | tf_op jit(solution)/shard_map/ppermute | solution.py:38
  669.0 4.6 collective-permute-done.5
  673.6 3.3 fusion.12
  (572 shorter events, 136.1 us)
Async XLA Ops:
  6.5 81.1 %copy-start = (bf16[64,64]{1,0:T(8,128)(2,1)S(1)}, bf16[64,64]{1,0:T(8,128)(2,1)}, u32[]{:S(2)}) copy-start(bf16[64,64]{1,0:T(8,128)(2,1)} %param.22) | copy-start | bytes 24580
  6.5 62.2 %all-gather.2.cloned.1.call-start = ((), (), s32[]{:S(2)}) async-start(), calls=%async_computation | async-start | bytes 10485760 | tf_op jit(solution)/shard_map/all_gather | solution.py:130
  68.7 389.4 %collective-permute-start.2 = (bf16[64,64,1024]{2,1,0:T(8,128)(2,1)}, bf16[64,64,1024]{2,1,0:T(8,128)(2,1)}, u32[]{:S(2)}, u32[]{:S(2)}) collective-permute-start(bf16[64,64,1024]{2,1,0:T(8,128)(2,1)} %all-gather.2.cloned.1.call-done), channel_id=1, source_target_pairs={{0,4},{4,8},{8,12},{12,16},{16,20},{20,24},{24,28},{1,5},{5,9},{9,... | collective-permute-start | bytes 25165832 | tf_op jit(solution)/shard_map/ppermute | solution.py:27
  71.8 386.3 %collective-permute-start.3 = (bf16[64,64,1024]{2,1,0:T(8,128)(2,1)}, bf16[64,64,1024]{2,1,0:T(8,128)(2,1)}, u32[]{:S(2)}, u32[]{:S(2)}) collective-permute-start(bf16[64,64,1024]{2,1,0:T(8,128)(2,1)} %all-gather.2.cloned.1.call-done), channel_id=1, source_target_pairs={{4,0},{8,4},{12,8},{16,12},{20,16},{24,20},{28,24},{5,1},{9,5},{13... | collective-permute-start | bytes 25165832 | tf_op jit(solution)/shard_map/ppermute | solution.py:30
  76.2 377.6 %collective-permute-start = (bf16[4,64,1024]{2,1,0:T(8,128)(2,1)S(1)}, bf16[4,64,1024]{2,1,0:T(8,128)(2,1)S(1)}, u32[]{:S(2)}, u32[]{:S(2)}) collective-permute-start(bf16[4,64,1024]{2,1,0:T(8,128)(2,1)S(1)} %bitcast_convert_fusion), channel_id=1, source_target_pairs={{0,4},{4,8},{8,12},{12,16},{16,20},{20,24},{24,28},{1,5},{5,9},{9,... | collective-permute-start | bytes 1572872 | tf_op jit(solution)/shard_map/ppermute | solution.py:27
  78.4 379.5 %collective-permute-start.1 = (bf16[4,64,1024]{2,1,0:T(8,128)(2,1)S(1)}, bf16[4,64,1024]{2,1,0:T(8,128)(2,1)S(1)}, u32[]{:S(2)}, u32[]{:S(2)}) collective-permute-start(bf16[4,64,1024]{2,1,0:T(8,128)(2,1)S(1)} %bitcast_convert_fusion), channel_id=1, source_target_pairs={{4,0},{8,4},{12,8},{16,12},{20,16},{24,20},{28,24},{5,1},{9,5},{13... | collective-permute-start | bytes 1572872 | tf_op jit(solution)/shard_map/ppermute | solution.py:30
  83.1 374.9 %copy-start.11 = (f32[6]{0:T(128)}, f32[6]{0:T(128)S(1)}, u32[]{:S(2)}) copy-start(f32[6]{0:T(128)S(1)} %compare_convert_fusion) | copy-start | bytes 76
  84.5 572.0 %collective-permute-start.6 = (bf16[1024]{0:T(1024)(128)(2,1)}, bf16[1024]{0:T(1024)(128)(2,1)S(1)}, u32[]{:S(2)}, u32[]{:S(2)}) collective-permute-start(bf16[1024]{0:T(1024)(128)(2,1)} %get-tuple-element.256), channel_id=1, source_target_pairs={{0,4},{4,8},{8,12},{12,16},{16,20},{20,24},{24,28},{1,5},{5,9},{9,... | collective-permute-start | bytes 6152 | tf_op jit(solution)/shard_map/ppermute | solution.py:38
  453.9 202.6 %collective-permute-start.7 = (bf16[1024]{0:T(1024)(128)(2,1)S(1)}, bf16[1024]{0:T(1024)(128)(2,1)}, u32[]{:S(2)}, u32[]{:S(2)}) collective-permute-start(bf16[1024]{0:T(1024)(128)(2,1)S(1)} %get-tuple-element.257), channel_id=1, source_target_pairs={{4,0},{8,4},{12,8},{16,12},{20,16},{24,20},{28,24},{5,1},{9,5},{13... | collective-permute-start | bytes 6152 | tf_op jit(solution)/shard_map/ppermute | solution.py:38
  458.1 17.7 %copy-start.6 = (bf16[64,36]{0,1:T(8,128)(2,1)S(1)}, bf16[64,36]{0,1:T(8,128)(2,1)}, u32[]{:S(2)}) copy-start(bf16[64,36]{0,1:T(8,128)(2,1)} %param.23) | copy-start | bytes 13828
  458.1 17.7 %copy-start.7 = (bf16[4,576]{1,0:T(4,128)(2,1)S(1)}, bf16[4,576]{1,0:T(4,128)(2,1)}, u32[]{:S(2)}) copy-start(bf16[4,576]{1,0:T(4,128)(2,1)} %param.26) | copy-start | bytes 13828
  458.1 17.7 %copy-start.8 = (f32[64]{0:T(128)S(1)}, f32[64]{0:T(128)}, u32[]{:S(2)}) copy-start(f32[64]{0:T(128)} %param.27) | copy-start | bytes 772
  458.1 17.7 %copy-start.9 = (f32[64]{0:T(128)S(1)}, f32[64]{0:T(128)}, u32[]{:S(2)}) copy-start(f32[64]{0:T(128)} %param.28) | copy-start | bytes 772
  458.1 17.7 %copy-start.10 = (f32[64]{0:T(128)S(1)}, f32[64]{0:T(128)}, u32[]{:S(2)}) copy-start(f32[64]{0:T(128)} %param.29) | copy-start | bytes 772
  475.8 2.7 copy-start.2
  494.5 2.3 copy-start.3
  496.7 2.7 copy-start.2
  518.0 2.7 copy-start.2
  539.3 2.7 copy-start.2
  560.5 2.7 copy-start.2
  581.8 2.7 copy-start.2
  644.1 32.8 %copy-start.1 = (bf16[64,64]{1,0:T(8,128)(2,1)S(1)}, bf16[64,64]{1,0:T(8,128)(2,1)}, u32[]{:S(2)}) copy-start(bf16[64,64]{1,0:T(8,128)(2,1)} %param.22) | copy-start | bytes 24580
  645.4 23.6 %collective-permute-start.4 = (bf16[4,64,1024]{2,1,0:T(8,128)(2,1)}, bf16[4,64,1024]{2,1,0:T(8,128)(2,1)}, u32[]{:S(2)}, u32[]{:S(2)}) collective-permute-start(bf16[4,64,1024]{2,1,0:T(8,128)(2,1)} %get-tuple-element.254), channel_id=1, source_target_pairs={{0,4},{4,8},{8,12},{12,16},{16,20},{20,24},{24,28},{1,5},{5,9},{9,... | collective-permute-start | bytes 1572872 | tf_op jit(solution)/shard_map/ppermute | solution.py:38
  647.3 26.2 %collective-permute-start.5 = (bf16[4,64,1024]{2,1,0:T(8,128)(2,1)}, bf16[4,64,1024]{2,1,0:T(8,128)(2,1)}, u32[]{:S(2)}, u32[]{:S(2)}) collective-permute-start(bf16[4,64,1024]{2,1,0:T(8,128)(2,1)} %get-tuple-element.255), channel_id=1, source_target_pairs={{4,0},{8,4},{12,8},{16,12},{20,16},{24,20},{28,24},{5,1},{9,5},{13... | collective-permute-start | bytes 1572872 | tf_op jit(solution)/shard_map/ppermute | solution.py:38
  (17 other events, 35.1 us)
Sparse Core Ops, SparseCore 0:
  8.9 59.7 all-gather.1
where the time goes:
time: 685 us; the launch traced here: 684 us
  waiting for transfers between devices  445 us (65%)
  other arithmetic  96.2 us (14%)
  local copies, waits for them, and re-layouts  50.1 us (7%)
  loops' own time  25.2 us (4%)
  matrix products  24.7 us (4%)
  starting transfers between devices  24.5 us (4%)
  between operations  18.3 us (3%)
    ppermute x2, waiting for transfers between devices, with_halo(): lax.ppermute(lax.slice_in_dim(block, block.shape[dim] - width, None, axis...  366 us
    all_gather x1, waiting for transfers between devices, body(): all_channels = lax.all_gather(features, 'member', axis=0, tiled=True)  61.5 us
    while x108, other arithmetic  27.5 us
    dot_general x24, matrix products, conv_same(): return jnp.dot(weight, stacked, preferred_element_type=jnp.float32)  24.5 us
    concatenate x2, other arithmetic, with_halo(): block = jnp.concatenate([low, block, high], axis=dim)  17.7 us
    ppermute x4, waiting for transfers between devices, from_behind(): return lax.ppermute(value, axis, pairs)  16.4 us
  transfers between devices with their start and end apart: 9, of which 4 were waited for; matrix products, arithmetic and copies ran while one was open for 24% of the time, Pallas kernels for 0%

commit v1 on v0

--- a/solution.py
+++ b/solution.py
@@ -40,9 +40,10 @@
 
 def plan_terms(timestep):
     betas_root = jnp.linspace(beta_first**0.5, beta_last**0.5, TRAIN_STEPS, dtype=jnp.float32)
-    alpha_bar = jnp.cumprod(1.0 - betas_root * betas_root)
-    current = alpha_bar[timestep[0]]
-    earlier = alpha_bar[timestep[0] - STRIDE]
+    kept = 1.0 - betas_root * betas_root
+    step = jnp.arange(TRAIN_STEPS, dtype=jnp.int32)
+    current = jnp.prod(jnp.where(step <= timestep[0], kept, 1.0))
+    earlier = jnp.prod(jnp.where(step <= timestep[0] - STRIDE, kept, 1.0))
     sigma_sq = eta_noise * eta_noise * (1.0 - earlier) / (1.0 - current) * (1.0 - current / earlier)
     return (current, earlier, sigma_sq)
 

time: 685 us -> 679 us (level)
  transfers between devices with their start and end apart: 9 -> 9, of which waited for: 4 -> 5; matrix products, arithmetic and copies ran while one was open for 24% -> 1% of each run, Pallas kernels for 0% -> 0%
where the time goes in v1:
time: 679 us; the launch traced here: 678 us
  waiting for transfers between devices  445 us (66%)
  other arithmetic  95.8 us (14%)
  local copies, waits for them, and re-layouts  44.6 us (7%)
  loops' own time  25.2 us (4%)
  matrix products  24.8 us (4%)
  starting transfers between devices  24.7 us (4%)
  between operations  18.3 us (3%)
    ppermute x2, waiting for transfers between devices, with_halo(): lax.ppermute(lax.slice_in_dim(block, block.shape[dim] - width, None, axis...  369 us
    all_gather x1, waiting for transfers between devices, body(): all_channels = lax.all_gather(features, 'member', axis=0, tiled=True)  61.5 us
    while x108, other arithmetic  27.5 us
    dot_general x24, matrix products, conv_same(): return jnp.dot(weight, stacked, preferred_element_type=jnp.float32)  24.6 us
    concatenate x2, other arithmetic, with_halo(): block = jnp.concatenate([low, block, high], axis=dim)  17.7 us
  transfers between devices with their start and end apart: 9, of which 5 were waited for; matrix products, arithmetic and copies ran while one was open for 1% of the time, Pallas kernels for 0%

profile of v1, /device:TPU:17, one launch (start us, length us, event | category | flops | bytes accessed | tf_op | source)
XLA Modules:
  0.0 678.3 jit_solution(9812453653305107138)
XLA Ops:
  7.3 61.5 %all-gather.2.cloned.1.call-done = bf16[64,64,1024]{2,1,0:T(8,128)(2,1)} async-done(((bf16[16,64,1024]{2,1,0:T(8,128)(2,1)}), bf16[64,64,1024]{2,1,0:T(8,128)(2,1)}) %all-gather.2.cloned.1.call-update) | async-done | bytes 8388624 | tf_op jit(solution)/shard_map/all_gather | solution.py:131
  68.7 3.1 collective-permute-start.2
  71.8 3.1 collective-permute-start.3
  76.2 2.2 collective-permute-start
  78.4 4.0 collective-permute-start.1
  84.8 369.1 %collective-permute-done = bf16[4,64,1024]{2,1,0:T(8,128)(2,1)S(1)} collective-permute-done((bf16[4,64,1024]{2,1,0:T(8,128)(2,1)S(1)}, bf16[4,64,1024]{2,1,0:T(8,128)(2,1)S(1)}, u32[]{:S(2)}, u32[]{:S(2)}) %collective-permute-start) | collective-permute-done | bytes 524320 | tf_op jit(solution)/shard_map/ppermute | solution.py:27
  453.9 2.5 collective-permute-done.1
  456.5 17.6 %pad_maximum_fusion = bf16[64,64,3072]{2,1,0:T(8,128)(2,1)} fusion(bf16[64,64,1024]{2,1,0:T(8,128)(2,1)} %collective-permute-done.3, bf16[64,64,1024]{2,1,0:T(8,128)(2,1)} %all-gather.2.cloned.1.call-done, bf16[64,64,1024]{2,1,0:T(8,128)(2,1)} %collective-permute-done.2), kind=kLoop, calls=%fused_computation.70 | loop fusion | flops 75497472 | bytes 50331648 | tf_op jit(solution)/shard_map/concatenate | solution.py:31
  474.2 127.3 %while.22 = (s32[]{:T(128)}, f32[6,4,4096]{2,1,0:T(4,128)}, s32[6]{0:T(128)S(1)}, bf16[4,64,3072]{2,1,0:T(8,128)(2,1)S(1)}, bf16[64,36]{0,1:T(8,128)(2,1)S(1)}, ...) while((s32[]{:T(128)}, f32[6,4,4096]{2,1,0:T(4,128)}, ...), condition=%wide.region_15.16_spmd, body=%wide.region_2.15_spmd.sunk | while | flops 663355456 | bytes 75635800 | solution.py:159
  477.4 1.6 dynamic-slice_convert_fusion.2
  498.3 2.0 dynamic-slice_convert_fusion.2
  519.6 2.0 dynamic-slice_convert_fusion.2
  540.8 2.0 dynamic-slice_convert_fusion.2
  562.1 2.0 dynamic-slice_convert_fusion.2
  583.4 2.0 dynamic-slice_convert_fusion.2
  601.9 36.7 %while.23 = (s32[]{:T(128)}, f32[4,64,3072]{2,1,0:T(8,128)S(1)}, s32[6]{0:T(128)S(1)}, f32[6]{0:T(128)S(1)}, f32[6,4,4096]{2,1,0:T(4,128)}, /*index=5*/s32[]{:T(128)}, s32[]{:T(128)}, s32[]{:T(128)}) while((s32[]{:T(128)}, f32[4,64,3072]{2,1,0:T(8,128)S(1)}, s32[6]{0:T(128)S(1)}, f32[6]{0:T(128)S(1)}, f32[6,4,4096]{2,1,0:T(4,128)}, ...), condition=%wide.region_17.18_spmd, body=%wide.region_16.17_spmd.sunk | while | flops 32773 | bytes 589983 | solution.py:167
  605.3 1.5 dynamic-slice_multiply_fusion.2
  639.8 2.2 collective-permute-start.4
  642.0 4.0 collective-permute-start.5
  646.0 1.9 collective-permute-start.6
  647.9 4.3 collective-permute-start.7
  657.0 6.7 collective-permute-done.6
  663.7 4.3 collective-permute-done.7
  668.1 3.3 fusion.12
  (563 shorter events, 131.9 us)
Async XLA Ops:
  6.5 78.0 %copy-start = (bf16[64,64]{1,0:T(8,128)(2,1)S(1)}, bf16[64,64]{1,0:T(8,128)(2,1)}, u32[]{:S(2)}) copy-start(bf16[64,64]{1,0:T(8,128)(2,1)} %param.22) | copy-start | bytes 24580
  6.5 62.2 %all-gather.2.cloned.1.call-start = ((), (), s32[]{:S(2)}) async-start(), calls=%async_computation | async-start | bytes 10485760 | tf_op jit(solution)/shard_map/all_gather | solution.py:131
  68.7 387.8 %collective-permute-start.2 = (bf16[64,64,1024]{2,1,0:T(8,128)(2,1)}, bf16[64,64,1024]{2,1,0:T(8,128)(2,1)}, u32[]{:S(2)}, u32[]{:S(2)}) collective-permute-start(bf16[64,64,1024]{2,1,0:T(8,128)(2,1)} %all-gather.2.cloned.1.call-done), channel_id=1, source_target_pairs={{0,4},{4,8},{8,12},{12,16},{16,20},{20,24},{24,28},{1,5},{5,9},{9,... | collective-permute-start | bytes 25165832 | tf_op jit(solution)/shard_map/ppermute | solution.py:27
  71.8 384.7 %collective-permute-start.3 = (bf16[64,64,1024]{2,1,0:T(8,128)(2,1)}, bf16[64,64,1024]{2,1,0:T(8,128)(2,1)}, u32[]{:S(2)}, u32[]{:S(2)}) collective-permute-start(bf16[64,64,1024]{2,1,0:T(8,128)(2,1)} %all-gather.2.cloned.1.call-done), channel_id=1, source_target_pairs={{4,0},{8,4},{12,8},{16,12},{20,16},{24,20},{28,24},{5,1},{9,5},{13... | collective-permute-start | bytes 25165832 | tf_op jit(solution)/shard_map/ppermute | solution.py:30
  76.2 377.6 %collective-permute-start = (bf16[4,64,1024]{2,1,0:T(8,128)(2,1)S(1)}, bf16[4,64,1024]{2,1,0:T(8,128)(2,1)S(1)}, u32[]{:S(2)}, u32[]{:S(2)}) collective-permute-start(bf16[4,64,1024]{2,1,0:T(8,128)(2,1)S(1)} %bitcast_convert_fusion), channel_id=1, source_target_pairs={{0,4},{4,8},{8,12},{12,16},{16,20},{20,24},{24,28},{1,5},{5,9},{9,... | collective-permute-start | bytes 1572872 | tf_op jit(solution)/shard_map/ppermute | solution.py:27
  78.4 377.9 %collective-permute-start.1 = (bf16[4,64,1024]{2,1,0:T(8,128)(2,1)S(1)}, bf16[4,64,1024]{2,1,0:T(8,128)(2,1)S(1)}, u32[]{:S(2)}, u32[]{:S(2)}) collective-permute-start(bf16[4,64,1024]{2,1,0:T(8,128)(2,1)S(1)} %bitcast_convert_fusion), channel_id=1, source_target_pairs={{4,0},{8,4},{12,8},{16,12},{20,16},{24,20},{28,24},{5,1},{9,5},{13... | collective-permute-start | bytes 1572872 | tf_op jit(solution)/shard_map/ppermute | solution.py:30
  456.4 17.7 %copy-start.6 = (bf16[64,36]{0,1:T(8,128)(2,1)S(1)}, bf16[64,36]{0,1:T(8,128)(2,1)}, u32[]{:S(2)}) copy-start(bf16[64,36]{0,1:T(8,128)(2,1)} %param.23) | copy-start | bytes 13828
  456.5 17.7 %copy-start.7 = (bf16[4,576]{1,0:T(4,128)(2,1)S(1)}, bf16[4,576]{1,0:T(4,128)(2,1)}, u32[]{:S(2)}) copy-start(bf16[4,576]{1,0:T(4,128)(2,1)} %param.26) | copy-start | bytes 13828
  456.5 17.7 %copy-start.8 = (f32[64]{0:T(128)S(1)}, f32[64]{0:T(128)}, u32[]{:S(2)}) copy-start(f32[64]{0:T(128)} %param.27) | copy-start | bytes 772
  456.5 17.7 %copy-start.9 = (f32[64]{0:T(128)S(1)}, f32[64]{0:T(128)}, u32[]{:S(2)}) copy-start(f32[64]{0:T(128)} %param.28) | copy-start | bytes 772
  456.5 17.7 %copy-start.10 = (f32[64]{0:T(128)S(1)}, f32[64]{0:T(128)}, u32[]{:S(2)}) copy-start(f32[64]{0:T(128)} %param.29) | copy-start | bytes 772
  474.2 2.7 copy-start.2
  492.8 2.3 copy-start.3
  495.1 2.7 copy-start.2
  514.1 2.3 copy-start.3
  516.4 2.7 copy-start.2
  537.7 2.7 copy-start.2
  558.9 2.7 copy-start.2
  580.2 2.7 copy-start.2
  638.5 32.9 %copy-start.1 = (bf16[64,64]{1,0:T(8,128)(2,1)S(1)}, bf16[64,64]{1,0:T(8,128)(2,1)}, u32[]{:S(2)}) copy-start(bf16[64,64]{1,0:T(8,128)(2,1)} %param.22) | copy-start | bytes 24580
  639.8 28.3 %collective-permute-start.4 = (bf16[4,64,1024]{2,1,0:T(8,128)(2,1)}, bf16[4,64,1024]{2,1,0:T(8,128)(2,1)}, u32[]{:S(2)}, u32[]{:S(2)}) collective-permute-start(bf16[4,64,1024]{2,1,0:T(8,128)(2,1)} %get-tuple-element.256), channel_id=1, source_target_pairs={{0,4},{4,8},{8,12},{12,16},{16,20},{20,24},{24,28},{1,5},{5,9},{9,... | collective-permute-start | bytes 1572872 | tf_op jit(solution)/shard_map/ppermute | solution.py:38
  642.0 26.1 %collective-permute-start.5 = (bf16[4,64,1024]{2,1,0:T(8,128)(2,1)}, bf16[4,64,1024]{2,1,0:T(8,128)(2,1)}, u32[]{:S(2)}, u32[]{:S(2)}) collective-permute-start(bf16[4,64,1024]{2,1,0:T(8,128)(2,1)} %get-tuple-element.257), channel_id=1, source_target_pairs={{4,0},{8,4},{12,8},{16,12},{20,16},{24,20},{28,24},{5,1},{9,5},{13... | collective-permute-start | bytes 1572872 | tf_op jit(solution)/shard_map/ppermute | solution.py:38
  646.0 17.7 %collective-permute-start.6 = (bf16[1024]{0:T(1024)(128)(2,1)S(1)}, bf16[1024]{0:T(1024)(128)(2,1)S(1)}, u32[]{:S(2)}, u32[]{:S(2)}) collective-permute-start(bf16[1024]{0:T(1024)(128)(2,1)S(1)} %get-tuple-element.258), channel_id=1, source_target_pairs={{0,4},{4,8},{8,12},{12,16},{16,20},{20,24},{24,28},{1,5},{5,9},{9,... | collective-permute-start | bytes 6152 | tf_op jit(solution)/shard_map/ppermute | solution.py:38
  647.9 20.1 %collective-permute-start.7 = (bf16[1024]{0:T(1024)(128)(2,1)S(1)}, bf16[1024]{0:T(1024)(128)(2,1)S(1)}, u32[]{:S(2)}, u32[]{:S(2)}) collective-permute-start(bf16[1024]{0:T(1024)(128)(2,1)S(1)} %get-tuple-element.259), channel_id=1, source_target_pairs={{4,0},{8,4},{12,8},{16,12},{20,16},{24,20},{28,24},{5,1},{9,5},{13... | collective-permute-start | bytes 6152 | tf_op jit(solution)/shard_map/ppermute | solution.py:38
  (16 other events, 32.9 us)
Sparse Core Ops, SparseCore 0:
  8.9 59.7 all-gather.1

commit v2 on v1

v2 whole, which is shorter than its diff:
```python
import math

import jax
import jax.numpy as jnp
from jax import lax
from jax.experimental import pallas as pl
from jax.experimental.pallas import tpu as pltpu
from jax.sharding import PartitionSpec as P

LAT = 4
WIN = 64
REACH = 1
TRAIN_STEPS = 1000
STRIDE = 20
GROUPS = 32


norm_epsilon = 1e-05
eta_noise = 0.5
beta_first = 0.00085
beta_last = 0.012


def plan_terms(timestep):
    betas_root = jnp.linspace(beta_first**0.5, beta_last**0.5, TRAIN_STEPS, dtype=jnp.float32)
    kept = 1.0 - betas_root * betas_root
    step = jnp.arange(TRAIN_STEPS, dtype=jnp.int32)
    current = jnp.prod(jnp.where(step <= timestep[0], kept, 1.0))
    earlier = jnp.prod(jnp.where(step <= timestep[0] - STRIDE, kept, 1.0))
    sigma_sq = eta_noise * eta_noise * (1.0 - earlier) / (1.0 - current) * (1.0 - current / earlier)
    return (current, earlier, sigma_sq)


def time_embed(timestep, time_weight):
    half_width = time_weight.shape[0] // 2
    freqs_row = jnp.exp(-math.log(10000.0) * jnp.arange(half_width, dtype=jnp.float32) / half_width)
    angles = timestep[0].astype(jnp.float32) * freqs_row
    embedding = jnp.concatenate([jnp.cos(angles), jnp.sin(angles)]).astype(jnp.bfloat16)
    return jax.nn.silu(
        jnp.dot(embedding[None, :], time_weight, preferred_element_type=jnp.float32)[0]
    )


def fold_taps(weight, cin, cin_pad, cout_pad):
    cout = weight.shape[0]
    folded = weight.reshape(cout, 3, 3, cin).transpose(2, 0, 1, 3)
    folded = jnp.pad(folded, ((0, 0), (0, cout_pad - cout), (0, 0), (0, cin_pad - cin)))
    return folded.reshape(3 * cout_pad, 3 * cin_pad)


def conv_cells(activation, folded, cout, row_first, row_last, cell):
    cells = activation.shape[1]
    above = jnp.where(row_first, 0.0, pltpu.roll(activation, 1, 1))
    below = jnp.where(row_last, 0.0, pltpu.roll(activation, cells - 1, 1))
    stacked = jnp.concatenate(
        [above.astype(jnp.bfloat16), activation.astype(jnp.bfloat16), below.astype(jnp.bfloat16)],
        axis=0,
    )
    parts = jnp.dot(folded, stacked, preferred_element_type=jnp.float32)
    left = jnp.where(cell < WIN, 0.0, pltpu.roll(parts[:cout], WIN, 1))
    right = jnp.where(cell >= cells - WIN, 0.0, pltpu.roll(parts[2 * cout :], cells - WIN, 1))
    return parts[cout : 2 * cout] + left + right


def norm_silu(hidden, gain):
    channels, cells = hidden.shape
    size = channels // GROUPS
    lane = (channels, 128)
    row = lax.broadcasted_iota(jnp.int32, lane, 0)

    def group_mean(values):
        total = jnp.broadcast_to(jnp.sum(values, axis=1, keepdims=True), lane)
        step = 1
        while step < size:
            up = pltpu.roll(total, channels - step, 0)
            down = pltpu.roll(total, step, 0)
            total = total + jnp.where((row // step) % 2 == 0, up, down)
            step *= 2
        return total[:, :1] / (size * cells)

    deviate = hidden - group_mean(hidden)
    spread_sq = group_mean(deviate * deviate)
    normed = deviate * (lax.rsqrt(spread_sq + norm_epsilon) * gain)
    return jax.nn.silu(normed).astype(jnp.bfloat16).astype(jnp.float32)


def window_kernel(feature_ref, latent_ref, in_ref, one_ref, two_ref, out_ref, column_ref, eps_ref):
    cells = WIN * WIN
    half = cells // 2
    cell = lax.broadcasted_iota(jnp.int32, (1, cells), 1)
    row = cell % WIN
    marks = (row == 0, row == WIN - 1, cell)
    members = feature_ref.shape[0]
    channels = one_ref.shape[0] // 3
    feature = jnp.concatenate(
        [
            jnp.concatenate([feature_ref[m, h] for m in range(members)], axis=0)
            for h in range(2)
        ],
        axis=1,
    ).astype(jnp.float32)
    latent_win = jnp.concatenate([latent_ref[0], latent_ref[1]], axis=1).astype(jnp.float32)
    gain_one, gain_two, gain_three, time_bias = (column_ref[:, k : k + 1] for k in range(4))
    hidden = conv_cells(latent_win, in_ref[...], channels, *marks) + feature
    act = norm_silu(hidden, gain_one)
    middle = conv_cells(act, one_ref[...], channels, *marks) + time_bias
    act = norm_silu(middle, gain_two)
    block_out = hidden + conv_cells(act, two_ref[...], channels, *marks)
    act = norm_silu(block_out, gain_three)
    eps = conv_cells(act, out_ref[...], out_ref.shape[0] // 3, *marks)
    eps_ref[0] = eps[:LAT, :half]
    eps_ref[1] = eps[:LAT, half:]


def denoise_windows(feature, latent_win, folded, columns):
    members, halves, share, half = feature.shape
    padded = latent_win.shape[1]
    whole = [pl.BlockSpec(f.shape, lambda s: (0, 0)) for f in (*folded, columns)]
    slots = halves // 2
    return pl.pallas_call(
        window_kernel,
        grid=(slots,),
        in_specs=[
            pl.BlockSpec((members, 2, share, half), lambda s: (0, s, 0, 0)),
            pl.BlockSpec((2, padded, half), lambda s: (s, 0, 0)),
            *whole,
        ],
        out_specs=pl.BlockSpec((2, LAT, half), lambda s: (s, 0, 0)),
        out_shape=jax.ShapeDtypeStruct((halves, LAT, half), jnp.float32),
        compiler_params=pltpu.CompilerParams(vmem_limit_bytes=50 * 2**20),
        cost_estimate=pl.CostEstimate(
            flops=slots * 2 * sum(f.size for f in folded) * 2 * half,
            bytes_accessed=2 * feature.size,
            transcendentals=0,
        ),
    )(feature, latent_win, *folded, columns)


def pick_kernel(wanted_ref, block_ref, *picked_refs):
    for which, picked_ref in enumerate(picked_refs):
        for k in range(picked_ref.shape[0]):
            picked_ref[k] = block_ref[wanted_ref[which, k]]


def pick_blocks(wanted, blocks):
    shape = jax.ShapeDtypeStruct((wanted.shape[1], *blocks.shape[1:]), blocks.dtype)
    return pl.pallas_call(
        pick_kernel,
        in_specs=[
            pl.BlockSpec(memory_space=pltpu.SMEM),
            pl.BlockSpec(memory_space=pltpu.VMEM),
        ],
        out_specs=[pl.BlockSpec(memory_space=pltpu.VMEM)] * wanted.shape[0],
        out_shape=[shape] * wanted.shape[0],
        compiler_params=pltpu.CompilerParams(vmem_limit_bytes=24 * 2**20),
    )(wanted, blocks)


def shift_tiles(value, by):
    count = lax.axis_size("tile")
    return lax.ppermute(
        value, "tile", [(i, i + by) for i in range(count) if 0 <= i + by < count]
    )


def by_blocks(array, half_win):
    channels, rows, width = array.shape
    split = array.reshape(channels, rows, width // half_win, half_win)
    return split.transpose(2, 0, 3, 1).reshape(width // half_win, channels, half_win * rows)


def denoise_update(state_now, eps_mean, noise_draw, current, earlier, sigma_sq):
    clean_est = (state_now - jnp.sqrt(1.0 - current) * eps_mean) / jnp.sqrt(current)
    return (
        jnp.sqrt(earlier) * clean_est
        + jnp.sqrt(1.0 - earlier - sigma_sq) * eps_mean
        + jnp.sqrt(sigma_sq) * noise_draw
    )


def body(
    latent,
    noise,
    features,
    slot_window,
    timestep,
    time_weight,
    in_weight,
    conv1_weight,
    conv2_weight,
    out_weight,
    norm1_gain,
    norm2_gain,
    norm3_gain,
):
    tile_width = latent.shape[-1]
    half_win = WIN // 2
    per_tile = tile_width // half_win
    tile_index = lax.axis_index("tile")
    slots_low = shift_tiles(slot_window + 1, 1) - 1
    slots_high = shift_tiles(slot_window + 1, -1) - 1

    def places(slots):
        start = slots - tile_index * per_tile
        return jnp.stack([start, start + 1], axis=1).reshape(-1)

    feature_blocks = by_blocks(features, half_win)
    latent_blocks = by_blocks(latent[0].astype(jnp.bfloat16), half_win)
    own = places(slot_window)
    low = places(slots_low)
    high = places(slots_high)

    wanted = jnp.clip(jnp.stack([own, low, high]), 0, per_tile - 1)
    mine = own[:, None, None]

    def listed_blocks(picked):
        from_high = shift_tiles(picked[1], -1)
        from_low = shift_tiles(picked[2], 1)
        return jnp.where(mine < 0, from_low, jnp.where(mine >= per_tile, from_high, picked[0]))

    feature_win = lax.all_gather(
        listed_blocks(pick_blocks(wanted, feature_blocks)), "member", axis=0
    )
    latent_win = listed_blocks(pick_blocks(wanted, latent_blocks))
    pad = 16 - LAT
    latent_win = jnp.pad(latent_win, ((0, 0), (0, pad), (0, 0)))
    current, earlier, sigma_sq = plan_terms(timestep)
    time_bias = time_embed(timestep, time_weight)
    channels = in_weight.shape[0]
    folded = (
        fold_taps(in_weight, LAT, LAT + pad, channels),
        fold_taps(conv1_weight, channels, channels, channels),
        fold_taps(conv2_weight, channels, channels, channels),
        fold_taps(out_weight, channels, channels, 8),
    )
    columns = jnp.stack([norm1_gain, norm2_gain, norm3_gain, time_bias] * 2, axis=1)
    eps = denoise_windows(feature_win, latent_win, folded, columns)
    halves = eps.shape[0]
    eps_link = eps.astype(jnp.bfloat16)
    eps_all = jnp.concatenate(
        [
            eps,
            shift_tiles(eps_link, 1).astype(jnp.float32),
            shift_tiles(eps_link, -1).astype(jnp.float32),
        ]
    )
    place = jnp.concatenate([own, low, high])
    listed = jnp.repeat(jnp.concatenate([slot_window, slots_low, slots_high]) >= 0, 2)
    block_ids = jnp.arange(per_tile, dtype=jnp.int32)
    hit = ((place[None, :] == block_ids[:, None]) & listed[None, :]).astype(jnp.float32)
    cover = jnp.sum(hit, axis=1)
    total = jnp.dot(
        hit,
        eps_all.reshape(3 * halves, -1),
        precision=lax.Precision.HIGHEST,
        preferred_element_type=jnp.float32,
    )
    eps_mean = total / jnp.maximum(cover, 1.0)[:, None]
    eps_mean = (
        eps_mean.reshape(per_tile, LAT, half_win, WIN)
        .transpose(1, 3, 0, 2)
        .reshape(LAT, WIN, tile_width)
    )
    return denoise_update(latent[0], eps_mean, noise[0], current, earlier, sigma_sq)[None]


def solution(mesh):
    placed = (
        P("member", None, None, "tile"),
        P("member", None, None, "tile"),
        P("member", None, "tile"),
        P("tile"),
        P(),
        P(),
        P(),
        P(),
        P(),
        P(),
        P(),
        P(),
        P(),
    )
    return jax.shard_map(
        body, mesh=mesh, in_specs=placed, out_specs=P("member", None, None, "tile"), check_vma=False
    )
```

time: 679 us -> 172 us (0.25)
  waiting for transfers between devices: 445 us -> 52.8 us
  other arithmetic: 95.8 us -> 7.69 us
  Pallas kernels: 0 us -> 35.7 us
  loops' own time: 25.2 us -> 0 us
  matrix products: 24.8 us -> 1.9 us
  local copies, waits for them, and re-layouts: 44.6 us -> 30.9 us
    ppermute x8, waiting for transfers between devices: 383 us -> 47.9 us  [shift_tiles(): lax.ppermute(value, 'tile', [(i, i + by) for i in range(count) if 0 <= i...]
    all_gather x1, waiting for transfers between devices: 61.5 us -> 4.85 us  [body(): lax.all_gather(listed_blocks(pick_blocks(wanted, feature_blocks)), 'membe...]
    pallas_call x0 -> x3, Pallas kernels: none -> 35.7 us  [the longest x1 33.2 us: denoise_windows(): pl.pallas_call(window_kernel, grid=(slots,), in_specs=[pl.BlockSpec((memb...]
    while x108 -> x0, other arithmetic: 27.5 us -> none
    another operation x2 -> x0, loops' own time: 25.2 us -> none  [the longest x1 12.7 us: body(): lax.scan(add_slot, jnp.zeros((LAT, WIN, ext_width), jnp.float32), (local_...]
    dot_general x24 -> x1, matrix products: 24.6 us -> 1.7 us  [body(): jnp.dot(hit, eps_all.reshape(3 * halves, -1), precision=lax.Precision.HIG...]
    concatenate x20 -> x2, other arithmetic: 21.6 us -> 0.55 us  [the longest x1 0.47 us: body(): jnp.concatenate([eps, shift_tiles(eps_link, 1).astype(jnp.float32), shift...]
    convert_element_type x26 -> x3, other arithmetic: 21 us -> 0.13 us  [the longest x1 0.08 us: body(): eps_link = eps.astype(jnp.bfloat16)]
  transfers between devices with their start and end apart: 9 -> 9, of which waited for: 5 -> 7; matrix products, arithmetic and copies ran while one was open for 1% -> 12% of each run, Pallas kernels for 0% -> 0%
where the time goes in v2:
time: 172 us; the launch traced here: 170 us
  waiting for transfers between devices  52.8 us (31%)
  Pallas kernels  35.7 us (21%)
  local copies, waits for them, and re-layouts  30.9 us (18%)
  starting transfers between devices  23.1 us (13%)
  between operations  18.1 us (11%)
  other arithmetic  7.69 us (4%)
  matrix products  1.9 us (1%)
    ppermute x8, waiting for transfers between devices, shift_tiles(): lax.ppermute(value, 'tile', [(i, i + by) for i in range(count) if 0 <= i...  47.9 us
    pallas_call x1, Pallas kernels, denoise_windows(): pl.pallas_call(window_kernel, grid=(slots,), in_specs=[pl.BlockSpec((memb...  33.2 us
    ppermute x8, starting transfers between devices, shift_tiles(): lax.ppermute(value, 'tile', [(i, i + by) for i in range(count) if 0 <= i...  23.1 us
    reshape x4, local copies, waits for them, and re-layouts, by_blocks(): split.transpose(2, 0, 3, 1)  10.7 us
    unnamed x31, local copies, waits for them, and re-layouts  7.54 us
    mul x3, local copies, waits for them, and re-layouts, denoise_update(): jnp.sqrt(1.0 - current) * eps_mean  5.82 us
    all_gather x1, waiting for transfers between devices, body(): lax.all_gather(listed_blocks(pick_blocks(wanted, feature_blocks)), 'membe...  4.85 us
    mul x3, local copies, waits for them, and re-layouts, denoise_update(): jnp.sqrt(1.0 - earlier - sigma_sq) * eps_mean  4.55 us
  transfers between devices with their start and end apart: 9, of which 7 were waited for; matrix products, arithmetic and copies ran while one was open for 12% of the time, Pallas kernels for 0%

profile of v2, /device:TPU:17, one launch (start us, length us, event | category | flops | bytes accessed | tf_op | source)
XLA Modules:
  0.0 170.1 jit_solution(15311646624762246169)
XLA Ops:
  7.2 3.0 %collective-permute-start.1 = (s32[6]{0:T(128)S(1)}, s32[6]{0:T(128)S(1)}, u32[]{:S(2)}, u32[]{:S(2)}) collective-permute-start(s32[6]{0:T(128)S(1)} %get-tuple-element.31), channel_id=1, source_target_pairs={{4,0},{8,4},{12,8},{16,12},{20,16},{24,20},{28,24},{5,1},{9,5},{13... | collective-permute-start | bytes 80 | tf_op jit(solution)/shard_map/ppermute | solution.py:161
  10.2 2.2 %collective-permute-start = (s32[6]{0:T(128)S(1)}, s32[6]{0:T(128)S(1)}, u32[]{:S(2)}, u32[]{:S(2)}) collective-permute-start(s32[6]{0:T(128)S(1)} %get-tuple-element.31), channel_id=1, source_target_pairs={{0,4},{4,8},{8,12},{12,16},{16,20},{20,24},{24,28},{1,5},{5,9},{9,... | collective-permute-start | bytes 80 | tf_op jit(solution)/shard_map/ppermute | solution.py:161
  12.7 4.8 %copy.118 = bf16[16,64,1024]{1,2,0:T(8,128)(2,1)} copy(bf16[16,64,1024]{2,1,0:T(8,128)(2,1)} %param.15) | data formatting | bytes 4194304 | tf_op args[2]
  17.5 6.7 %reshape.126 = bf16[32,16,2048]{2,0,1:T(8,128)(2,1)} reshape(bf16[32,16,32,64]{3,2,0,1:T(8,128)(2,1)} %bitcast.74) | data formatting | bytes 4194304 | tf_op jit(solution)/shard_map/reshape | solution.py:169
  24.2 2.7 %copy.134.block_ref = bf16[32,16,2048]{2,1,0:T(8,128)(2,1)S(1)} copy(bf16[32,16,2048]{2,0,1:T(8,128)(2,1)} %reshape.126) | data formatting | bytes 4194304 | tf_op jit(solution)/shard_map/reshape | solution.py:169
  29.2 4.0 %collective-permute-start.2 = (bf16[12,16,2048]{2,1,0:T(8,128)(2,1)}, bf16[12,16,2048]{2,1,0:T(8,128)(2,1)S(1)}, u32[]{:S(2)}, u32[]{:S(2)}) collective-permute-start(bf16[12,16,2048]{2,1,0:T(8,128)(2,1)} %get-tuple-element.11), channel_id=1, source_target_pairs={{0,4},{4,8},{8,12},{12,16},{16,20},{20,24},{24,28},{1,5},{5,9},{9,... | collective-permute-start | bytes 2359304 | tf_op jit(solution)/shard_map/ppermute | solution.py:161
  33.3 2.1 %collective-permute-start.3 = (bf16[12,16,2048]{2,1,0:T(8,128)(2,1)}, bf16[12,16,2048]{2,1,0:T(8,128)(2,1)S(1)}, u32[]{:S(2)}, u32[]{:S(2)}) collective-permute-start(bf16[12,16,2048]{2,1,0:T(8,128)(2,1)} %get-tuple-element.12), channel_id=1, source_target_pairs={{4,0},{8,4},{12,8},{16,12},{20,16},{24,20},{28,24},{5,1},{9,5},{13... | collective-permute-start | bytes 2359304 | tf_op jit(solution)/shard_map/ppermute | solution.py:161
  35.5 30.5 %collective-permute-done.2 = bf16[12,16,2048]{2,1,0:T(8,128)(2,1)S(1)} collective-permute-done((bf16[12,16,2048]{2,1,0:T(8,128)(2,1)}, bf16[12,16,2048]{2,1,0:T(8,128)(2,1)S(1)}, u32[]{:S(2)}, u32[]{:S(2)}) %collective-permute-start.2) | collective-permute-done | bytes 786464 | tf_op jit(solution)/shard_map/ppermute | solution.py:161
  66.0 2.5 %collective-permute-done.3 = bf16[12,16,2048]{2,1,0:T(8,128)(2,1)S(1)} collective-permute-done((bf16[12,16,2048]{2,1,0:T(8,128)(2,1)}, bf16[12,16,2048]{2,1,0:T(8,128)(2,1)S(1)}, u32[]{:S(2)}, u32[]{:S(2)}) %collective-permute-start.3) | collective-permute-done | bytes 786464 | tf_op jit(solution)/shard_map/ppermute | solution.py:161
  69.4 2.4 %select_select_fusion = bf16[12,16,2048]{2,1,0:T(8,128)(2,1)} fusion(bf16[12,16,2048]{2,1,0:T(8,128)(2,1)S(1)} %collective-permute-done.2, bf16[12,16,2048]{2,1,0:T(8,128)(2,1)} %copy-done.3, bf16[12,16,2048]{2,1,0:T(8,128)(2,1)S(1)} %get-tuple-element.13, pred[12]{0:T(512)(128)(4,1)S(1)} %get-tuple-element.28, pred[12]{0:T(512)(128)(4,1)S(1)} %get-tuple-element.27), kind=kLoop, calls=%fused_computation.4 | loop fusion | flops 786432 | bytes 3145752 | tf_op jit(solution)/shard_map/jit(_where)/select_n | solution.py:219
  81.6 1.9 %collective-permute-start.4 = (bf16[12,4,2048]{2,1,0:T(4,128)(2,1)S(1)}, bf16[12,4,2048]{2,1,0:T(4,128)(2,1)S(1)}, u32[]{:S(2)}, u32[]{:S(2)}) collective-permute-start(bf16[12,4,2048]{2,1,0:T(4,128)(2,1)S(1)} %get-tuple-element.14), channel_id=1, source_target_pairs={{0,4},{4,8},{8,12},{12,16},{16,20},{20,24},{24,28},{1,5},{5,9},{9,... | collective-permute-start | bytes 589832 | tf_op jit(solution)/shard_map/ppermute | solution.py:161
  83.6 4.4 %collective-permute-start.5 = (bf16[12,4,2048]{2,1,0:T(4,128)(2,1)S(1)}, bf16[12,4,2048]{2,1,0:T(4,128)(2,1)S(1)}, u32[]{:S(2)}, u32[]{:S(2)}) collective-permute-start(bf16[12,4,2048]{2,1,0:T(4,128)(2,1)S(1)} %get-tuple-element.15), channel_id=1, source_target_pairs={{4,0},{8,4},{12,8},{16,12},{20,16},{24,20},{28,24},{5,1},{9,5},{13... | collective-permute-start | bytes 589832 | tf_op jit(solution)/shard_map/ppermute | solution.py:161
  88.2 2.2 %collective-permute-done.4 = bf16[12,4,2048]{2,1,0:T(4,128)(2,1)S(1)} collective-permute-done((bf16[12,4,2048]{2,1,0:T(4,128)(2,1)S(1)}, bf16[12,4,2048]{2,1,0:T(4,128)(2,1)S(1)}, u32[]{:S(2)}, u32[]{:S(2)}) %collective-permute-start.4) | collective-permute-done | bytes 196640 | tf_op jit(solution)/shard_map/ppermute | solution.py:161
  90.4 5.2 %collective-permute-done.5 = bf16[12,4,2048]{2,1,0:T(4,128)(2,1)S(1)} collective-permute-done((bf16[12,4,2048]{2,1,0:T(4,128)(2,1)S(1)}, bf16[12,4,2048]{2,1,0:T(4,128)(2,1)S(1)}, u32[]{:S(2)}, u32[]{:S(2)}) %collective-permute-start.5) | collective-permute-done | bytes 196640 | tf_op jit(solution)/shard_map/ppermute | solution.py:161
  96.0 4.9 %all-gather.3.cloned.1.call-done = bf16[48,16,2048]{2,1,0:T(8,128)(2,1)} async-done(((bf16[12,16,2048]{2,1,0:T(8,128)(2,1)}), bf16[48,16,2048]{2,1,0:T(8,128)(2,1)}) %all-gather.3.cloned.1.call-update) | async-done | bytes 3145744 | tf_op jit(solution)/shard_map/all_gather | solution.py:221
  100.8 33.2 %shard_map.129 = f32[12,4,2048]{2,1,0:T(4,128)S(1)} custom-call(bf16[4,12,16,2048]{3,2,1,0:T(8,128)(2,1)} %bitcast.90, bf16[12,16,2048]{2,1,0:T(8,128)(2,1)S(1)} %pad.12.latent_ref, bf16[192,48]{1,0:T(8,128)(2,1)S(1)} %copy.128.in_ref, bf16[192,192]{1,0:T(8,128)(2,1)S(1)} %reshape.117.one_ref, bf16[192,192]{1,0:T(8,128)(2,1)S(1)} %reshape.119.two_ref, ...), custom_call_target="tpu_custom_call" | custom-call | flops 4303355904 | bytes 3145728 | tf_op jit(solution)/shard_map/pallas_call | solution.py:120
  134.1 3.1 %collective-permute-start.7 = (bf16[12,4,2048]{2,1,0:T(4,128)(2,1)S(1)}, bf16[12,4,2048]{2,1,0:T(4,128)(2,1)S(1)}, u32[]{:S(2)}, u32[]{:S(2)}) collective-permute-start(bf16[12,4,2048]{2,1,0:T(4,128)(2,1)S(1)} %convert_element_type.33), channel_id=1, source_target_pairs={{4,0},{8,4},{12,8},{16,12},{20,16},{24,20},{28,24},{5,1},{9,5},{13... | collective-permute-start | bytes 589832 | tf_op jit(solution)/shard_map/ppermute | solution.py:161
  137.2 2.2 %collective-permute-start.6 = (bf16[12,4,2048]{2,1,0:T(4,128)(2,1)S(1)}, bf16[12,4,2048]{2,1,0:T(4,128)(2,1)S(1)}, u32[]{:S(2)}, u32[]{:S(2)}) collective-permute-start(bf16[12,4,2048]{2,1,0:T(4,128)(2,1)S(1)} %convert_element_type.33), channel_id=1, source_target_pairs={{0,4},{4,8},{8,12},{12,16},{16,20},{20,24},{24,28},{1,5},{5,9},{9,... | collective-permute-start | bytes 589832 | tf_op jit(solution)/shard_map/ppermute | solution.py:161
  139.4 2.8 %collective-permute-done.7 = bf16[12,4,2048]{2,1,0:T(4,128)(2,1)S(1)} collective-permute-done((bf16[12,4,2048]{2,1,0:T(4,128)(2,1)S(1)}, bf16[12,4,2048]{2,1,0:T(4,128)(2,1)S(1)}, u32[]{:S(2)}, u32[]{:S(2)}) %collective-permute-start.7) | collective-permute-done | bytes 196640 | tf_op jit(solution)/shard_map/ppermute | solution.py:161
  142.3 4.7 %collective-permute-done.6 = bf16[12,4,2048]{2,1,0:T(4,128)(2,1)S(1)} collective-permute-done((bf16[12,4,2048]{2,1,0:T(4,128)(2,1)S(1)}, bf16[12,4,2048]{2,1,0:T(4,128)(2,1)S(1)}, u32[]{:S(2)}, u32[]{:S(2)}) %collective-permute-start.6) | collective-permute-done | bytes 196640 | tf_op jit(solution)/shard_map/ppermute | solution.py:161
  152.6 2.2 %copy.133 = f32[1,4,64,1024]{3,2,1,0:T(8,128)S(1)} copy(f32[1,4,64,1024]{2,3,1,0:T(8,128)} %bitcast.75) | data formatting | bytes 2097152 | tf_op jit(solution)/shard_map/mul | solution.py:176
  154.8 2.0 %mul.117 = f32[32,4,32,64]{3,2,1,0:T(8,128)S(1)} reshape(f32[32,8192]{1,0:T(8,128)} %get-tuple-element.19) | data formatting | bytes 2097152 | tf_op jit(solution)/shard_map/mul | solution.py:173
  158.3 2.3 %copy.131 = f32[1,4,64,1024]{3,2,1,0:T(8,128)S(1)} copy(f32[1,4,64,1024]{2,3,1,0:T(8,128)} %bitcast.76) | data formatting | bytes 2097152 | tf_op jit(solution)/shard_map/mul | solution.py:173
  160.6 2.6 %multiply_add_fusion = f32[1,4,64,1024]{3,2,1,0:T(8,128)} fusion(f32[1,4,64,1024]{3,2,1,0:T(8,128)} %param.14, f32[1,4,64,1024]{3,2,1,0:T(8,128)S(1)} %copy.133, f32[1,4,64,1024]{3,2,1,0:T(8,128)S(1)} %copy-done.2, f32[1,4,64,1024]{3,2,1,0:T(8,128)S(1)} %copy.131, f32[]{:T(128)S(6)} %sqrt.19, f32[]{:T(128)S(6)} %sqrt.17, f32[]{:T(128)S(6)} %sqrt.15), kind=kLoop, calls=%fused_computation.3 | loop fusion | flops 1572864 | bytes 5242892 | tf_op jit(solution)/shard_map/add | solution.py:175
  (89 shorter events, 17.3 us)
Async XLA Ops:
  6.5 73.7 %copy-start = (bf16[64,64]{1,0:T(8,128)(2,1)S(1)}, bf16[64,64]{1,0:T(8,128)(2,1)}, u32[]{:S(2)}) copy-start(bf16[64,64]{1,0:T(8,128)(2,1)} %param.18) | copy-start | bytes 24580
  6.5 94.3 %all-gather.3.cloned.1.call-start = ((), (), s32[]{:S(2)}) async-start(), calls=%async_computation | async-start | bytes 3932160 | tf_op jit(solution)/shard_map/all_gather | solution.py:221
  7.2 19.7 %collective-permute-start.1 = (s32[6]{0:T(128)S(1)}, s32[6]{0:T(128)S(1)}, u32[]{:S(2)}, u32[]{:S(2)}) collective-permute-start(s32[6]{0:T(128)S(1)} %get-tuple-element.31), channel_id=1, source_target_pairs={{4,0},{8,4},{12,8},{16,12},{20,16},{24,20},{28,24},{5,1},{9,5},{13... | collective-permute-start | bytes 80 | tf_op jit(solution)/shard_map/ppermute | solution.py:161
  10.2 16.8 %collective-permute-start = (s32[6]{0:T(128)S(1)}, s32[6]{0:T(128)S(1)}, u32[]{:S(2)}, u32[]{:S(2)}) collective-permute-start(s32[6]{0:T(128)S(1)} %get-tuple-element.31), channel_id=1, source_target_pairs={{0,4},{4,8},{8,12},{12,16},{16,20},{20,24},{24,28},{1,5},{5,9},{9,... | collective-permute-start | bytes 80 | tf_op jit(solution)/shard_map/ppermute | solution.py:161
  29.2 36.8 %collective-permute-start.2 = (bf16[12,16,2048]{2,1,0:T(8,128)(2,1)}, bf16[12,16,2048]{2,1,0:T(8,128)(2,1)S(1)}, u32[]{:S(2)}, u32[]{:S(2)}) collective-permute-start(bf16[12,16,2048]{2,1,0:T(8,128)(2,1)} %get-tuple-element.11), channel_id=1, source_target_pairs={{0,4},{4,8},{8,12},{12,16},{16,20},{20,24},{24,28},{1,5},{5,9},{9,... | collective-permute-start | bytes 2359304 | tf_op jit(solution)/shard_map/ppermute | solution.py:161
  33.3 35.3 %collective-permute-start.3 = (bf16[12,16,2048]{2,1,0:T(8,128)(2,1)}, bf16[12,16,2048]{2,1,0:T(8,128)(2,1)S(1)}, u32[]{:S(2)}, u32[]{:S(2)}) collective-permute-start(bf16[12,16,2048]{2,1,0:T(8,128)(2,1)} %get-tuple-element.12), channel_id=1, source_target_pairs={{4,0},{8,4},{12,8},{16,12},{20,16},{24,20},{28,24},{5,1},{9,5},{13... | collective-permute-start | bytes 2359304 | tf_op jit(solution)/shard_map/ppermute | solution.py:161
  68.5 0.9 copy-start.3
  69.4 7.4 %copy-start.1 = (f32[1,4,64,1024]{3,2,1,0:T(8,128)S(1)}, f32[1,4,64,1024]{3,2,1,0:T(8,128)}, u32[]{:S(2)}) copy-start(f32[1,4,64,1024]{3,2,1,0:T(8,128)} %param.13) | copy-start | bytes 3145732
  77.3 1.3 copy-start.6
  77.3 1.6 copy-start.4
  78.2 1.3 copy-start.5
  78.2 1.8 %copy-start.7 = (bf16[4,576]{1,0:T(4,128)(2,1)S(1)}, bf16[4,576]{1,0:T(4,128)(2,1)}, u32[]{:S(2)}) copy-start(bf16[4,576]{1,0:T(4,128)(2,1)} %param.22) | copy-start | bytes 13828
  78.6 1.8 %copy-start.8 = (f32[64]{0:T(128)S(1)}, f32[64]{0:T(128)}, u32[]{:S(2)}) copy-start(f32[64]{0:T(128)} %param.23) | copy-start | bytes 772
  78.6 1.8 %copy-start.9 = (f32[64]{0:T(128)S(1)}, f32[64]{0:T(128)}, u32[]{:S(2)}) copy-start(f32[64]{0:T(128)} %param.24) | copy-start | bytes 772
  78.7 1.8 %copy-start.10 = (f32[64]{0:T(128)S(1)}, f32[64]{0:T(128)}, u32[]{:S(2)}) copy-start(f32[64]{0:T(128)} %param.25) | copy-start | bytes 772
  78.7 2.1 %copy-start.11 = (s32[6]{0:T(128)S(1)}, s32[6]{0:T(128)}, u32[]{:S(2)}) copy-start(s32[6]{0:T(128)} %param.16) | copy-start | bytes 76
  81.6 8.8 %collective-permute-start.4 = (bf16[12,4,2048]{2,1,0:T(4,128)(2,1)S(1)}, bf16[12,4,2048]{2,1,0:T(4,128)(2,1)S(1)}, u32[]{:S(2)}, u32[]{:S(2)}) collective-permute-start(bf16[12,4,2048]{2,1,0:T(4,128)(2,1)S(1)} %get-tuple-element.14), channel_id=1, source_target_pairs={{0,4},{4,8},{8,12},{12,16},{16,20},{20,24},{24,28},{1,5},{5,9},{9,... | collective-permute-start | bytes 589832 | tf_op jit(solution)/shard_map/ppermute | solution.py:161
  83.6 12.0 %collective-permute-start.5 = (bf16[12,4,2048]{2,1,0:T(4,128)(2,1)S(1)}, bf16[12,4,2048]{2,1,0:T(4,128)(2,1)S(1)}, u32[]{:S(2)}, u32[]{:S(2)}) collective-permute-start(bf16[12,4,2048]{2,1,0:T(4,128)(2,1)S(1)} %get-tuple-element.15), channel_id=1, source_target_pairs={{4,0},{8,4},{12,8},{16,12},{20,16},{24,20},{28,24},{5,1},{9,5},{13... | collective-permute-start | bytes 589832 | tf_op jit(solution)/shard_map/ppermute | solution.py:161
  134.1 8.1 %collective-permute-start.7 = (bf16[12,4,2048]{2,1,0:T(4,128)(2,1)S(1)}, bf16[12,4,2048]{2,1,0:T(4,128)(2,1)S(1)}, u32[]{:S(2)}, u32[]{:S(2)}) collective-permute-start(bf16[12,4,2048]{2,1,0:T(4,128)(2,1)S(1)} %convert_element_type.33), channel_id=1, source_target_pairs={{4,0},{8,4},{12,8},{16,12},{20,16},{24,20},{28,24},{5,1},{9,5},{13... | collective-permute-start | bytes 589832 | tf_op jit(solution)/shard_map/ppermute | solution.py:161
  137.2 9.8 %collective-permute-start.6 = (bf16[12,4,2048]{2,1,0:T(4,128)(2,1)S(1)}, bf16[12,4,2048]{2,1,0:T(4,128)(2,1)S(1)}, u32[]{:S(2)}, u32[]{:S(2)}) collective-permute-start(bf16[12,4,2048]{2,1,0:T(4,128)(2,1)S(1)} %convert_element_type.33), channel_id=1, source_target_pairs={{0,4},{4,8},{8,12},{12,16},{16,20},{20,24},{24,28},{1,5},{5,9},{9,... | collective-permute-start | bytes 589832 | tf_op jit(solution)/shard_map/ppermute | solution.py:161
  158.3 2.3 %copy-start.2 = (f32[1,4,64,1024]{3,2,1,0:T(8,128)S(1)}, f32[1,4,64,1024]{3,2,1,0:T(8,128)}, u32[]{:S(2)}) copy-start(f32[1,4,64,1024]{3,2,1,0:T(8,128)} %param.13) | copy-start | bytes 3145732
Sparse Core Ops, SparseCore 0:
  71.9 28.8 all-gather.2

commit v3 on v2

--- a/solution.py
+++ b/solution.py
@@ -1,3 +1,4 @@
+import functools
 import math
 
 import jax
@@ -13,6 +14,7 @@
 TRAIN_STEPS = 1000
 STRIDE = 20
 GROUPS = 32
+PIECES = 2
 
 
 norm_epsilon = 1e-05
@@ -136,24 +138,35 @@
     )(feature, latent_win, *folded, columns)
 
 
-def pick_kernel(wanted_ref, block_ref, *picked_refs):
-    for which, picked_ref in enumerate(picked_refs):
-        for k in range(picked_ref.shape[0]):
-            picked_ref[k] = block_ref[wanted_ref[which, k]]
-
-
-def pick_blocks(wanted, blocks):
-    shape = jax.ShapeDtypeStruct((wanted.shape[1], *blocks.shape[1:]), blocks.dtype)
-    return pl.pallas_call(
-        pick_kernel,
-        in_specs=[
-            pl.BlockSpec(memory_space=pltpu.SMEM),
-            pl.BlockSpec(memory_space=pltpu.VMEM),
-        ],
-        out_specs=[pl.BlockSpec(memory_space=pltpu.VMEM)] * wanted.shape[0],
-        out_shape=[shape] * wanted.shape[0],
+def pick_kernel(sizes, wanted_ref, *refs):
+    source_refs, picked_refs = refs[: len(sizes)], refs[len(sizes) :]
+    kinds = wanted_ref.shape[0]
+    for index, picked_ref in enumerate(picked_refs):
+        piece, kind = divmod(index, kinds)
+        count = picked_ref.shape[0]
+        for k in range(count):
+            block = wanted_ref[kind, piece * count + k]
+            low = 0
+            for source_ref, size in zip(source_refs, sizes):
+                at = pl.multiple_of(block * size, size)
+                picked_ref[k, :, low : low + size] = source_ref[:, pl.ds(at, size)]
+                low += size
+
+
+def pick_blocks(wanted, sources, pieces, sizes):
+    kinds, count = wanted.shape
+    rows = sources[0].shape[0]
+    shape = jax.ShapeDtypeStruct((count // pieces, rows, sum(sizes)), sources[0].dtype)
+    outs = kinds * pieces
+    picked = pl.pallas_call(
+        functools.partial(pick_kernel, sizes),
+        in_specs=[pl.BlockSpec(memory_space=pltpu.SMEM)]
+        + [pl.BlockSpec(memory_space=pltpu.VMEM)] * len(sources),
+        out_specs=[pl.BlockSpec(memory_space=pltpu.VMEM)] * outs,
+        out_shape=[shape] * outs,
         compiler_params=pltpu.CompilerParams(vmem_limit_bytes=24 * 2**20),
-    )(wanted, blocks)
+    )(wanted, *sources)
+    return [picked[p * kinds : (p + 1) * kinds] for p in range(pieces)]
 
 
 def shift_tiles(value, by):
@@ -163,10 +176,8 @@
     )
 
 
-def by_blocks(array, half_win):
-    channels, rows, width = array.shape
-    split = array.reshape(channels, rows, width // half_win, half_win)
-    return split.transpose(2, 0, 3, 1).reshape(width // half_win, channels, half_win * rows)
+def by_columns(array):
+    return array.transpose(0, 2, 1).reshape(array.shape[0], -1)
 
 
 def denoise_update(state_now, eps_mean, noise_draw, current, earlier, sigma_sq):
@@ -204,26 +215,41 @@
         start = slots - tile_index * per_tile
         return jnp.stack([start, start + 1], axis=1).reshape(-1)
 
-    feature_blocks = by_blocks(features, half_win)
-    latent_blocks = by_blocks(latent[0].astype(jnp.bfloat16), half_win)
+    pieces = math.gcd(slot_window.shape[0], PIECES)
+    feature_cells = by_columns(features)
+    latent_cells = by_columns(latent[0].astype(jnp.bfloat16))
     own = places(slot_window)
     low = places(slots_low)
     high = places(slots_high)
 
     wanted = jnp.clip(jnp.stack([own, low, high]), 0, per_tile - 1)
-    mine = own[:, None, None]
-
-    def listed_blocks(picked):
+    mine = jnp.split(own[:, None, None], pieces)
+    half = half_win * WIN
+
+    def listed_blocks(piece, picked):
         from_high = shift_tiles(picked[1], -1)
         from_low = shift_tiles(picked[2], 1)
-        return jnp.where(mine < 0, from_low, jnp.where(mine >= per_tile, from_high, picked[0]))
-
-    feature_win = lax.all_gather(
-        listed_blocks(pick_blocks(wanted, feature_blocks)), "member", axis=0
-    )
-    latent_win = listed_blocks(pick_blocks(wanted, latent_blocks))
+        at = mine[piece]
+        return jnp.where(at < 0, from_low, jnp.where(at >= per_tile, from_high, picked[0]))
+
+    share = features.shape[0]
+    folds = share // LAT
+    thin = half // folds
+    latent_cells = (
+        latent_cells.reshape(LAT, per_tile, folds, thin)
+        .transpose(2, 0, 1, 3)
+        .reshape(share, per_tile * thin)
+    )
     pad = 16 - LAT
-    latent_win = jnp.pad(latent_win, ((0, 0), (0, pad), (0, 0)))
+    feature_wins, latent_wins = [], []
+    picks = pick_blocks(wanted, (feature_cells, latent_cells), pieces, (half, thin))
+    for piece, picked in enumerate(picks):
+        both = listed_blocks(piece, picked)
+        feature_wins.append(lax.all_gather(both[:, :, :half], "member", axis=0))
+        latent_win = both[:, :, half:].reshape(-1, folds, LAT, thin).transpose(0, 2, 1, 3)
+        latent_wins.append(
+            jnp.pad(latent_win.reshape(-1, LAT, half), ((0, 0), (0, pad), (0, 0)))
+        )
     current, earlier, sigma_sq = plan_terms(timestep)
     time_bias = time_embed(timestep, time_weight)
     channels = in_weight.shape[0]
@@ -234,16 +260,21 @@
         fold_taps(out_weight, channels, channels, 8),
     )
     columns = jnp.stack([norm1_gain, norm2_gain, norm3_gain, time_bias] * 2, axis=1)
-    eps = denoise_windows(feature_win, latent_win, folded, columns)
-    halves = eps.shape[0]
-    eps_link = eps.astype(jnp.bfloat16)
+    eps = jnp.concatenate(
+        [
+            denoise_windows(feature_win, latent_win, folded, columns)
+            for feature_win, latent_win in zip(feature_wins, latent_wins)
+        ]
+    )
+    link = eps.astype(jnp.bfloat16)
     eps_all = jnp.concatenate(
         [
             eps,
-            shift_tiles(eps_link, 1).astype(jnp.float32),
-            shift_tiles(eps_link, -1).astype(jnp.float32),
+            shift_tiles(link, 1).astype(jnp.float32),
+            shift_tiles(link, -1).astype(jnp.float32),
         ]
     )
+    halves = own.shape[0]
     place = jnp.concatenate([own, low, high])
     listed = jnp.repeat(jnp.concatenate([slot_window, slots_low, slots_high]) >= 0, 2)
     block_ids = jnp.arange(per_tile, dtype=jnp.int32)
@@ -261,6 +292,7 @@
         .transpose(1, 3, 0, 2)
         .reshape(LAT, WIN, tile_width)
     )
+    eps_mean = lax.optimization_barrier(eps_mean)
     return denoise_update(latent[0], eps_mean, noise[0], current, earlier, sigma_sq)[None]
 
 

time: 172 us -> 168 us (0.977)
  waiting for transfers between devices: 52.8 us -> 47.2 us
  local copies, waits for them, and re-layouts: 30.9 us -> 34.4 us
  starting transfers between devices: 23.1 us -> 25.3 us
    mul x6 -> x0, local copies, waits for them, and re-layouts: 10.4 us -> none  [the longest x3 5.82 us: denoise_update(): jnp.sqrt(1.0 - current) * eps_mean]
    all_gather x1 -> x2, waiting for transfers between devices: 4.85 us -> 0.04 us  [body(): feature_wins.append(lax.all_gather(both[:, :, :half], 'member', axis=0))]
    transpose x0 -> x2, local copies, waits for them, and re-layouts: none -> 4.4 us  [the longest x1 3.11 us: by_columns(): return array.transpose(0, 2, 1).reshape(array.shape[0], -1)]
    unnamed x31 -> x48, local copies, waits for them, and re-layouts: 7.54 us -> 11.7 us
    broadcast_in_dim x0 -> x1, local copies, waits for them, and re-layouts: none -> 3.15 us  [body(): denoise_update(latent[0], eps_mean, noise[0], current, earlier, sigma_sq)]
    add x1 -> x0, other arithmetic: 2.64 us -> none  [denoise_update(): jnp.sqrt(earlier) * clean_est]
    ppermute x8, starting transfers between devices: 23.1 us -> 25.2 us  [shift_tiles(): lax.ppermute(value, 'tile', [(i, i + by) for i in range(count) if 0 <= i...]
    broadcast_in_dim x0 -> x1, other arithmetic: none -> 1.91 us  [body(): denoise_update(latent[0], eps_mean, noise[0], current, earlier, sigma_sq)]
  transfers between devices with their start and end apart: 9 -> 10, of which waited for: 7 -> 6; matrix products, arithmetic and copies ran while one was open for 12% -> 13% of each run, Pallas kernels for 0% -> 10%
where the time goes in v3:
time: 168 us; the launch traced here: 167 us
  waiting for transfers between devices  47.2 us (28%)
  local copies, waits for them, and re-layouts  34.4 us (20%)
  Pallas kernels  34.1 us (20%)
  starting transfers between devices  25.3 us (15%)
  between operations  18.6 us (11%)
  other arithmetic  7.1 us (4%)
    ppermute x8, waiting for transfers between devices, shift_tiles(): lax.ppermute(value, 'tile', [(i, i + by) for i in range(count) if 0 <= i...  47.1 us
    pallas_call x2, Pallas kernels, denoise_windows(): pl.pallas_call(window_kernel, grid=(slots,), in_specs=[pl.BlockSpec((memb...  32.3 us
    ppermute x8, starting transfers between devices, shift_tiles(): lax.ppermute(value, 'tile', [(i, i + by) for i in range(count) if 0 <= i...  25.2 us
    unnamed x48, local copies, waits for them, and re-layouts  11.7 us
    reshape x1, local copies, waits for them, and re-layouts, by_columns(): return array.transpose(0, 2, 1).reshape(array.shape[0], -1)  4.72 us
    reshape x2, local copies, waits for them, and re-layouts, body(): eps_mean.reshape(per_tile, LAT, half_win, WIN).transpose(1, 3, 0, 2)  4.15 us
  transfers between devices with their start and end apart: 10, of which 6 were waited for; matrix products, arithmetic and copies ran while one was open for 13% of the time, Pallas kernels for 10%

profile of v3, /device:TPU:17, one launch (start us, length us, event | category | flops | bytes accessed | tf_op | source)
XLA Modules:
  0.0 167.4 jit_solution(1376577046161942855)
XLA Ops:
  7.2 3.1 %collective-permute-start = (s32[6]{0:T(128)S(1)}, s32[6]{0:T(128)S(1)}, u32[]{:S(2)}, u32[]{:S(2)}) collective-permute-start(s32[6]{0:T(128)S(1)} %get-tuple-element.31), channel_id=1, source_target_pairs={{0,4},{4,8},{8,12},{12,16},{16,20},{20,24},{24,28},{1,5},{5,9},{9,... | collective-permute-start | bytes 80 | tf_op jit(solution)/shard_map/ppermute | solution.py:174
  10.4 3.0 %collective-permute-start.1 = (s32[6]{0:T(128)S(1)}, s32[6]{0:T(128)S(1)}, u32[]{:S(2)}, u32[]{:S(2)}) collective-permute-start(s32[6]{0:T(128)S(1)} %get-tuple-element.31), channel_id=1, source_target_pairs={{4,0},{8,4},{12,8},{16,12},{20,16},{24,20},{28,24},{5,1},{9,5},{13... | collective-permute-start | bytes 80 | tf_op jit(solution)/shard_map/ppermute | solution.py:174
  13.6 1.8 %copy.102 = f32[1,4,64,1024]{2,3,1,0:T(8,128)S(1)} copy(f32[1,4,64,1024]{3,2,1,0:T(8,128)} %param.13) | data formatting | bytes 2097152 | tf_op args[0]
  18.7 3.1 %copy.110 = bf16[16,1024,64]{2,1,0:T(8,128)(2,1)} copy(bf16[16,1024,64]{1,2,0:T(8,128)(2,1)S(1)} %bitcast.95) | data formatting | bytes 4194304 | tf_op jit(solution)/shard_map/transpose | solution.py:180
  21.8 4.7 %reshape.120.refs_0_ = bf16[16,65536]{1,0:T(8,128)(2,1)S(1)} reshape(bf16[16,1024,64]{2,1,0:T(8,128)(2,1)} %copy.110) | data formatting | bytes 4194304 | tf_op jit(solution)/shard_map/reshape | solution.py:180
  31.1 2.4 %collective-permute-start.2 = (bf16[6,16,2560]{2,1,0:T(8,128)(2,1)}, bf16[6,16,2560]{2,1,0:T(8,128)(2,1)S(1)}, u32[]{:S(2)}, u32[]{:S(2)}) collective-permute-start(bf16[6,16,2560]{2,1,0:T(8,128)(2,1)} %get-tuple-element.11), channel_id=1, source_target_pairs={{0,4},{4,8},{8,12},{12,16},{16,20},{20,24},{24,28},{1,5},{5,9},{9,... | collective-permute-start | bytes 1474568 | tf_op jit(solution)/shard_map/ppermute | solution.py:174
  33.5 3.9 %collective-permute-start.3 = (bf16[6,16,2560]{2,1,0:T(8,128)(2,1)}, bf16[6,16,2560]{2,1,0:T(8,128)(2,1)S(1)}, u32[]{:S(2)}, u32[]{:S(2)}) collective-permute-start(bf16[6,16,2560]{2,1,0:T(8,128)(2,1)} %get-tuple-element.12), channel_id=1, source_target_pairs={{4,0},{8,4},{12,8},{16,12},{20,16},{24,20},{28,24},{5,1},{9,5},{13... | collective-permute-start | bytes 1474568 | tf_op jit(solution)/shard_map/ppermute | solution.py:174
  37.9 15.7 %collective-permute-done.2 = bf16[6,16,2560]{2,1,0:T(8,128)(2,1)S(1)} collective-permute-done((bf16[6,16,2560]{2,1,0:T(8,128)(2,1)}, bf16[6,16,2560]{2,1,0:T(8,128)(2,1)S(1)}, u32[]{:S(2)}, u32[]{:S(2)}) %collective-permute-start.2) | collective-permute-done | bytes 491552 | tf_op jit(solution)/shard_map/ppermute | solution.py:174
  53.6 4.3 %collective-permute-done.3 = bf16[6,16,2560]{2,1,0:T(8,128)(2,1)S(1)} collective-permute-done((bf16[6,16,2560]{2,1,0:T(8,128)(2,1)}, bf16[6,16,2560]{2,1,0:T(8,128)(2,1)S(1)}, u32[]{:S(2)}, u32[]{:S(2)}) %collective-permute-start.3) | collective-permute-done | bytes 491552 | tf_op jit(solution)/shard_map/ppermute | solution.py:174
  60.0 1.9 %collective-permute-start.4 = (bf16[6,16,2560]{2,1,0:T(8,128)(2,1)S(1)}, bf16[6,16,2560]{2,1,0:T(8,128)(2,1)S(1)}, u32[]{:S(2)}, u32[]{:S(2)}) collective-permute-start(bf16[6,16,2560]{2,1,0:T(8,128)(2,1)S(1)} %copy-done.7), channel_id=1, source_target_pairs={{0,4},{4,8},{8,12},{12,16},{16,20},{20,24},{24,28},{1,5},{5,9},{9,... | collective-permute-start | bytes 1474568 | tf_op jit(solution)/shard_map/ppermute | solution.py:174
  62.0 4.4 %collective-permute-start.5 = (bf16[6,16,2560]{2,1,0:T(8,128)(2,1)S(1)}, bf16[6,16,2560]{2,1,0:T(8,128)(2,1)S(1)}, u32[]{:S(2)}, u32[]{:S(2)}) collective-permute-start(bf16[6,16,2560]{2,1,0:T(8,128)(2,1)S(1)} %copy-done.5), channel_id=1, source_target_pairs={{4,0},{8,4},{12,8},{16,12},{20,16},{24,20},{28,24},{5,1},{9,5},{13... | collective-permute-start | bytes 1474568 | tf_op jit(solution)/shard_map/ppermute | solution.py:174
  66.8 16.1 %collective-permute-done.4 = bf16[6,16,2560]{2,1,0:T(8,128)(2,1)S(1)} collective-permute-done((bf16[6,16,2560]{2,1,0:T(8,128)(2,1)S(1)}, bf16[6,16,2560]{2,1,0:T(8,128)(2,1)S(1)}, u32[]{:S(2)}, u32[]{:S(2)}) %collective-permute-start.4) | collective-permute-done | bytes 491552 | tf_op jit(solution)/shard_map/ppermute | solution.py:174
  82.9 3.6 %collective-permute-done.5 = bf16[6,16,2560]{2,1,0:T(8,128)(2,1)S(1)} collective-permute-done((bf16[6,16,2560]{2,1,0:T(8,128)(2,1)S(1)}, bf16[6,16,2560]{2,1,0:T(8,128)(2,1)S(1)}, u32[]{:S(2)}, u32[]{:S(2)}) %collective-permute-start.5) | collective-permute-done | bytes 491552 | tf_op jit(solution)/shard_map/ppermute | solution.py:174
  96.7 1.9 %copy.128 = f32[1,4,64,1024]{2,3,1,0:T(8,128)S(1)} copy(f32[1,4,64,1024]{3,2,1,0:T(8,128)} %param.14) | data formatting | bytes 2097152 | tf_op args[1]
  101.0 16.2 %shard_map.128 = f32[6,4,2048]{2,1,0:T(4,128)S(1)} custom-call(bf16[4,6,16,2048]{3,2,1,0:T(8,128)(2,1)S(1)} %bitcast.91, bf16[6,16,2048]{2,1,0:T(8,128)(2,1)S(1)} %pad.15.latent_ref, bf16[192,48]{1,0:T(8,128)(2,1)S(1)} %copy.120.in_ref, bf16[192,192]{1,0:T(8,128)(2,1)S(1)} %reshape.127.one_ref, bf16[192,192]{1,0:T(8,128)(2,1)S(1)} %reshape.129.two_ref, ...), custom_call_target="tpu_custom_call" | custom-call | flops 2151677952 | bytes 1572864 | tf_op jit(solution)/shard_map/pallas_call | solution.py:122
  118.7 16.2 %shard_map.129 = f32[6,4,2048]{2,1,0:T(4,128)S(1)} custom-call(bf16[4,6,16,2048]{3,2,1,0:T(8,128)(2,1)S(1)} %bitcast.92, bf16[6,16,2048]{2,1,0:T(8,128)(2,1)S(1)} %pad.18.latent_ref, bf16[192,48]{1,0:T(8,128)(2,1)S(1)} %copy.120.in_ref, bf16[192,192]{1,0:T(8,128)(2,1)S(1)} %reshape.127.one_ref, bf16[192,192]{1,0:T(8,128)(2,1)S(1)} %reshape.129.two_ref, ...), custom_call_target="tpu_custom_call" | custom-call | flops 2151677952 | bytes 1572864 | tf_op jit(solution)/shard_map/pallas_call | solution.py:122
  135.0 2.1 %collective-permute-start.6 = (bf16[12,4,2048]{2,1,0:T(4,128)(2,1)S(1)}, bf16[12,4,2048]{2,1,0:T(4,128)(2,1)S(1)}, u32[]{:S(2)}, u32[]{:S(2)}) collective-permute-start(bf16[12,4,2048]{2,1,0:T(4,128)(2,1)S(1)} %pad_maximum_fusion.1), channel_id=1, source_target_pairs={{0,4},{4,8},{8,12},{12,16},{16,20},{20,24},{24,28},{1,5},{5,9},{9,... | collective-permute-start | bytes 589832 | tf_op jit(solution)/shard_map/ppermute | solution.py:174
  137.2 4.3 %collective-permute-start.7 = (bf16[12,4,2048]{2,1,0:T(4,128)(2,1)S(1)}, bf16[12,4,2048]{2,1,0:T(4,128)(2,1)S(1)}, u32[]{:S(2)}, u32[]{:S(2)}) collective-permute-start(bf16[12,4,2048]{2,1,0:T(4,128)(2,1)S(1)} %pad_maximum_fusion.1), channel_id=1, source_target_pairs={{4,0},{8,4},{12,8},{16,12},{20,16},{24,20},{28,24},{5,1},{9,5},{13... | collective-permute-start | bytes 589832 | tf_op jit(solution)/shard_map/ppermute | solution.py:174
  141.5 2.4 %collective-permute-done.6 = bf16[12,4,2048]{2,1,0:T(4,128)(2,1)S(1)} collective-permute-done((bf16[12,4,2048]{2,1,0:T(4,128)(2,1)S(1)}, bf16[12,4,2048]{2,1,0:T(4,128)(2,1)S(1)}, u32[]{:S(2)}, u32[]{:S(2)}) %collective-permute-start.6) | collective-permute-done | bytes 196640 | tf_op jit(solution)/shard_map/ppermute | solution.py:174
  143.9 5.0 %collective-permute-done.7 = bf16[12,4,2048]{2,1,0:T(4,128)(2,1)S(1)} collective-permute-done((bf16[12,4,2048]{2,1,0:T(4,128)(2,1)S(1)}, bf16[12,4,2048]{2,1,0:T(4,128)(2,1)S(1)}, u32[]{:S(2)}, u32[]{:S(2)}) %collective-permute-start.7) | collective-permute-done | bytes 196640 | tf_op jit(solution)/shard_map/ppermute | solution.py:174
  151.1 2.2 %reshape.135 = f32[32,4,32,64]{3,2,1,0:T(8,128)} reshape(f32[32,8192]{1,0:T(8,128)S(1)} %convolution_divide_fusion) | data formatting | bytes 2097152 | tf_op jit(solution)/shard_map/reshape | solution.py:291
  153.3 2.0 %copy.127 = f32[32,4,32,64]{3,2,0,1:T(8,128)S(1)} copy(f32[32,4,32,64]{3,2,1,0:T(8,128)} %reshape.135) | data formatting | bytes 2097152 | tf_op jit(solution)/shard_map/reshape | solution.py:291
  155.5 1.9 %fusion = f32[1,4,64,1024]{2,3,1,0:T(8,128)} fusion(f32[1,4,64,1024]{2,3,1,0:T(8,128)S(1)} %copy-done.9, f32[1,4,64,1024]{2,3,1,0:T(8,128)S(1)} %copy.128, f32[4,64,1024]{1,2,0:T(8,128)S(1)} %bitcast.93, f32[]{:T(128)S(6)} %sqrt.19, f32[]{:T(128)S(6)} %sqrt.18, f32[]{:T(128)S(6)} %sqrt.17, f32[]{:T(128)S(6)} %sqrt.16, f32[]{:T(128)S(6)} %sqrt.15), kind=kLoop, calls=%fused_computation.2 | loop fusion | flops 2097152 | bytes 4194324 | tf_op jit(solution)/shard_map/broadcast_in_dim | solution.py:296
  157.4 3.1 %copy.129 = f32[1,4,64,1024]{3,2,1,0:T(8,128)} copy(f32[1,4,64,1024]{2,3,1,0:T(8,128)} %fusion) | data formatting | bytes 2097152 | tf_op jit(solution)/shard_map/broadcast_in_dim | solution.py:296
  (128 shorter events, 23.5 us)
Async XLA Ops:
  6.5 88.2 %copy-start = (bf16[64,64]{1,0:T(8,128)(2,1)S(1)}, bf16[64,64]{1,0:T(8,128)(2,1)}, u32[]{:S(2)}) copy-start(bf16[64,64]{1,0:T(8,128)(2,1)} %param.18) | copy-start | bytes 24580
  6.5 93.1 %all-gather.5.cloned.1.call-start = ((), (), s32[]{:S(2)}) async-start(), calls=%async_computation | async-start | bytes 1966080 | tf_op jit(solution)/shard_map/all_gather | solution.py:248
  7.2 19.3 %collective-permute-start = (s32[6]{0:T(128)S(1)}, s32[6]{0:T(128)S(1)}, u32[]{:S(2)}, u32[]{:S(2)}) collective-permute-start(s32[6]{0:T(128)S(1)} %get-tuple-element.31), channel_id=1, source_target_pairs={{0,4},{4,8},{8,12},{12,16},{16,20},{20,24},{24,28},{1,5},{5,9},{9,... | collective-permute-start | bytes 80 | tf_op jit(solution)/shard_map/ppermute | solution.py:174
  10.4 16.4 %collective-permute-start.1 = (s32[6]{0:T(128)S(1)}, s32[6]{0:T(128)S(1)}, u32[]{:S(2)}, u32[]{:S(2)}) collective-permute-start(s32[6]{0:T(128)S(1)} %get-tuple-element.31), channel_id=1, source_target_pairs={{4,0},{8,4},{12,8},{16,12},{20,16},{24,20},{28,24},{5,1},{9,5},{13... | collective-permute-start | bytes 80 | tf_op jit(solution)/shard_map/ppermute | solution.py:174
  15.4 1.5 copy-start.8
  17.0 1.7 %copy-start.10 = (bf16[16,64,1024]{2,1,0:T(8,128)(2,1)S(1)}, bf16[16,64,1024]{2,1,0:T(8,128)(2,1)}, u32[]{:S(2)}) copy-start(bf16[16,64,1024]{2,1,0:T(8,128)(2,1)} %param.15) | copy-start | bytes 6291460
  31.1 28.9 %copy-start.7 = (bf16[6,16,2560]{2,1,0:T(8,128)(2,1)S(1)}, bf16[6,16,2560]{2,1,0:T(8,128)(2,1)}, u32[]{:S(2)}) copy-start(bf16[6,16,2560]{2,1,0:T(8,128)(2,1)} %copy-done.6) | copy-start | bytes 1474564
  31.1 30.9 %copy-start.5 = (bf16[6,16,2560]{2,1,0:T(8,128)(2,1)S(1)}, bf16[6,16,2560]{2,1,0:T(8,128)(2,1)}, u32[]{:S(2)}) copy-start(bf16[6,16,2560]{2,1,0:T(8,128)(2,1)} %copy-done.4) | copy-start | bytes 1474564
  31.1 22.5 %collective-permute-start.2 = (bf16[6,16,2560]{2,1,0:T(8,128)(2,1)}, bf16[6,16,2560]{2,1,0:T(8,128)(2,1)S(1)}, u32[]{:S(2)}, u32[]{:S(2)}) collective-permute-start(bf16[6,16,2560]{2,1,0:T(8,128)(2,1)} %get-tuple-element.11), channel_id=1, source_target_pairs={{0,4},{4,8},{8,12},{12,16},{16,20},{20,24},{24,28},{1,5},{5,9},{9,... | collective-permute-start | bytes 1474568 | tf_op jit(solution)/shard_map/ppermute | solution.py:174
  33.5 24.4 %collective-permute-start.3 = (bf16[6,16,2560]{2,1,0:T(8,128)(2,1)}, bf16[6,16,2560]{2,1,0:T(8,128)(2,1)S(1)}, u32[]{:S(2)}, u32[]{:S(2)}) collective-permute-start(bf16[6,16,2560]{2,1,0:T(8,128)(2,1)} %get-tuple-element.12), channel_id=1, source_target_pairs={{4,0},{8,4},{12,8},{16,12},{20,16},{24,20},{28,24},{5,1},{9,5},{13... | collective-permute-start | bytes 1474568 | tf_op jit(solution)/shard_map/ppermute | solution.py:174
  59.1 35.9 %copy-start.16 = (f32[64]{0:T(128)S(1)}, f32[64]{0:T(128)}, u32[]{:S(2)}) copy-start(f32[64]{0:T(128)} %param.23) | copy-start | bytes 772
  59.1 35.9 %copy-start.17 = (f32[64]{0:T(128)S(1)}, f32[64]{0:T(128)}, u32[]{:S(2)}) copy-start(f32[64]{0:T(128)} %param.24) | copy-start | bytes 772
  59.1 35.9 %copy-start.18 = (f32[64]{0:T(128)S(1)}, f32[64]{0:T(128)}, u32[]{:S(2)}) copy-start(f32[64]{0:T(128)} %param.25) | copy-start | bytes 772
  59.1 36.0 %copy-start.12 = (bf16[64,576]{1,0:T(8,128)(2,1)S(1)}, bf16[64,576]{1,0:T(8,128)(2,1)}, u32[]{:S(2)}) copy-start(bf16[64,576]{1,0:T(8,128)(2,1)} %param.20) | copy-start | bytes 221188
  60.0 35.7 %copy-start.13 = (bf16[64,576]{1,0:T(8,128)(2,1)S(1)}, bf16[64,576]{1,0:T(8,128)(2,1)}, u32[]{:S(2)}) copy-start(bf16[64,576]{1,0:T(8,128)(2,1)} %param.21) | copy-start | bytes 221188
  60.0 57.3 %all-gather.7.cloned.1.call-start = ((), (), s32[]{:S(2)}) async-start(), calls=%async_computation.1 | async-start | bytes 1966080 | tf_op jit(solution)/shard_map/all_gather | solution.py:248
  60.0 22.9 %collective-permute-start.4 = (bf16[6,16,2560]{2,1,0:T(8,128)(2,1)S(1)}, bf16[6,16,2560]{2,1,0:T(8,128)(2,1)S(1)}, u32[]{:S(2)}, u32[]{:S(2)}) collective-permute-start(bf16[6,16,2560]{2,1,0:T(8,128)(2,1)S(1)} %copy-done.7), channel_id=1, source_target_pairs={{0,4},{4,8},{8,12},{12,16},{16,20},{20,24},{24,28},{1,5},{5,9},{9,... | collective-permute-start | bytes 1474568 | tf_op jit(solution)/shard_map/ppermute | solution.py:174
  62.0 24.5 %collective-permute-start.5 = (bf16[6,16,2560]{2,1,0:T(8,128)(2,1)S(1)}, bf16[6,16,2560]{2,1,0:T(8,128)(2,1)S(1)}, u32[]{:S(2)}, u32[]{:S(2)}) collective-permute-start(bf16[6,16,2560]{2,1,0:T(8,128)(2,1)S(1)} %copy-done.5), channel_id=1, source_target_pairs={{4,0},{8,4},{12,8},{16,12},{20,16},{24,20},{28,24},{5,1},{9,5},{13... | collective-permute-start | bytes 1474568 | tf_op jit(solution)/shard_map/ppermute | solution.py:174
  87.3 8.8 %copy-start.14 = (bf16[64,36]{0,1:T(8,128)(2,1)S(1)}, bf16[64,36]{0,1:T(8,128)(2,1)}, u32[]{:S(2)}) copy-start(bf16[64,36]{0,1:T(8,128)(2,1)} %param.19) | copy-start | bytes 13828
  88.5 7.9 %copy-start.15 = (bf16[4,576]{1,0:T(4,128)(2,1)S(1)}, bf16[4,576]{1,0:T(4,128)(2,1)}, u32[]{:S(2)}) copy-start(bf16[4,576]{1,0:T(4,128)(2,1)} %param.22) | copy-start | bytes 13828
  95.8 2.9 %copy-start.19 = (s32[6]{0:T(128)S(1)}, s32[6]{0:T(128)}, u32[]{:S(2)}) copy-start(s32[6]{0:T(128)} %param.16) | copy-start | bytes 76
  135.0 8.8 %collective-permute-start.6 = (bf16[12,4,2048]{2,1,0:T(4,128)(2,1)S(1)}, bf16[12,4,2048]{2,1,0:T(4,128)(2,1)S(1)}, u32[]{:S(2)}, u32[]{:S(2)}) collective-permute-start(bf16[12,4,2048]{2,1,0:T(4,128)(2,1)S(1)} %pad_maximum_fusion.1), channel_id=1, source_target_pairs={{0,4},{4,8},{8,12},{12,16},{16,20},{20,24},{24,28},{1,5},{5,9},{9,... | collective-permute-start | bytes 589832 | tf_op jit(solution)/shard_map/ppermute | solution.py:174
  137.2 11.7 %collective-permute-start.7 = (bf16[12,4,2048]{2,1,0:T(4,128)(2,1)S(1)}, bf16[12,4,2048]{2,1,0:T(4,128)(2,1)S(1)}, u32[]{:S(2)}, u32[]{:S(2)}) collective-permute-start(bf16[12,4,2048]{2,1,0:T(4,128)(2,1)S(1)} %pad_maximum_fusion.1), channel_id=1, source_target_pairs={{4,0},{8,4},{12,8},{16,12},{20,16},{24,20},{28,24},{5,1},{9,5},{13... | collective-permute-start | bytes 589832 | tf_op jit(solution)/shard_map/ppermute | solution.py:174
  153.3 2.2 %copy-start.9 = (f32[1,4,64,1024]{2,3,1,0:T(8,128)S(1)}, f32[1,4,64,1024]{2,3,1,0:T(8,128)}, u32[]{:S(2)}) copy-start(f32[1,4,64,1024]{2,3,1,0:T(8,128)} %copy-done.8) | copy-start | bytes 3145732
  (6 other events, 6.0 us)
Sparse Core Ops, SparseCore 0:
  60.1 19.9 all-gather.4
  89.4 20.1 all-gather.6

commit v4 on v3

--- a/solution.py
+++ b/solution.py
@@ -101,7 +101,13 @@
         ],
         axis=1,
     ).astype(jnp.float32)
-    latent_win = jnp.concatenate([latent_ref[0], latent_ref[1]], axis=1).astype(jnp.float32)
+    packed = [latent_ref[h].astype(jnp.float32) for h in range(2)]
+    folds = packed[0].shape[0] // LAT
+    latent_win = jnp.concatenate(
+        [p[LAT * q : LAT * (q + 1)] for p in packed for q in range(folds)], axis=1
+    )
+    spare = in_ref.shape[1] // 3 - LAT
+    latent_win = jnp.concatenate([latent_win, jnp.zeros((spare, cells), jnp.float32)], axis=0)
     gain_one, gain_two, gain_three, time_bias = (column_ref[:, k : k + 1] for k in range(4))
     hidden = conv_cells(latent_win, in_ref[...], channels, *marks) + feature
     act = norm_silu(hidden, gain_one)
@@ -116,7 +122,6 @@
 
 def denoise_windows(feature, latent_win, folded, columns):
     members, halves, share, half = feature.shape
-    padded = latent_win.shape[1]
     whole = [pl.BlockSpec(f.shape, lambda s: (0, 0)) for f in (*folded, columns)]
     slots = halves // 2
     return pl.pallas_call(
@@ -124,7 +129,7 @@
         grid=(slots,),
         in_specs=[
             pl.BlockSpec((members, 2, share, half), lambda s: (0, s, 0, 0)),
-            pl.BlockSpec((2, padded, half), lambda s: (s, 0, 0)),
+            pl.BlockSpec((2, *latent_win.shape[1:]), lambda s: (s, 0, 0)),
             *whole,
         ],
         out_specs=pl.BlockSpec((2, LAT, half), lambda s: (s, 0, 0)),
@@ -246,10 +251,7 @@
     for piece, picked in enumerate(picks):
         both = listed_blocks(piece, picked)
         feature_wins.append(lax.all_gather(both[:, :, :half], "member", axis=0))
-        latent_win = both[:, :, half:].reshape(-1, folds, LAT, thin).transpose(0, 2, 1, 3)
-        latent_wins.append(
-            jnp.pad(latent_win.reshape(-1, LAT, half), ((0, 0), (0, pad), (0, 0)))
-        )
+        latent_wins.append(both[:, :, half:])
     current, earlier, sigma_sq = plan_terms(timestep)
     time_bias = time_embed(timestep, time_weight)
     channels = in_weight.shape[0]

time: 168 us -> 167 us (level)
  no operation moved by 1% of the time
where the time goes in v4:
time: 167 us; the launch traced here: 166 us
  waiting for transfers between devices  47.1 us (28%)
  local copies, waits for them, and re-layouts  34.2 us (20%)
  Pallas kernels  33.8 us (20%)
  starting transfers between devices  25.3 us (15%)
  between operations  18.6 us (11%)
  other arithmetic  6.02 us (4%)
    ppermute x8, waiting for transfers between devices, shift_tiles(): lax.ppermute(value, 'tile', [(i, i + by) for i in range(count) if 0 <= i...  47.1 us
    pallas_call x2, Pallas kernels, denoise_windows(): pl.pallas_call(window_kernel, grid=(slots,), in_specs=[pl.BlockSpec((memb...  32.1 us
    ppermute x8, starting transfers between devices, shift_tiles(): lax.ppermute(value, 'tile', [(i, i + by) for i in range(count) if 0 <= i...  25.2 us
    unnamed x48, local copies, waits for them, and re-layouts  10.9 us
    reshape x1, local copies, waits for them, and re-layouts, by_columns(): return array.transpose(0, 2, 1).reshape(array.shape[0], -1)  4.72 us
    reshape x2, local copies, waits for them, and re-layouts, body(): eps_mean.reshape(per_tile, LAT, half_win, WIN).transpose(1, 3, 0, 2)  4.15 us
  transfers between devices with their start and end apart: 10, of which 6 were waited for; matrix products, arithmetic and copies ran while one was open for 13% of the time, Pallas kernels for 10%

profile of v4, /device:TPU:17, one launch (start us, length us, event | category | flops | bytes accessed | tf_op | source)
XLA Modules:
  0.0 166.0 jit_solution(16333693193348255349)
XLA Ops:
  7.2 3.1 %collective-permute-start = (s32[6]{0:T(128)S(1)}, s32[6]{0:T(128)S(1)}, u32[]{:S(2)}, u32[]{:S(2)}) collective-permute-start(s32[6]{0:T(128)S(1)} %get-tuple-element.31), channel_id=1, source_target_pairs={{0,4},{4,8},{8,12},{12,16},{16,20},{20,24},{24,28},{1,5},{5,9},{9,... | collective-permute-start | bytes 80 | tf_op jit(solution)/shard_map/ppermute | solution.py:179
  10.4 3.0 %collective-permute-start.1 = (s32[6]{0:T(128)S(1)}, s32[6]{0:T(128)S(1)}, u32[]{:S(2)}, u32[]{:S(2)}) collective-permute-start(s32[6]{0:T(128)S(1)} %get-tuple-element.31), channel_id=1, source_target_pairs={{4,0},{8,4},{12,8},{16,12},{20,16},{24,20},{28,24},{5,1},{9,5},{13... | collective-permute-start | bytes 80 | tf_op jit(solution)/shard_map/ppermute | solution.py:179
  13.6 1.8 %copy.96 = f32[1,4,64,1024]{2,3,1,0:T(8,128)S(1)} copy(f32[1,4,64,1024]{3,2,1,0:T(8,128)} %param.13) | data formatting | bytes 2097152 | tf_op args[0]
  18.7 3.1 %copy.104 = bf16[16,1024,64]{2,1,0:T(8,128)(2,1)} copy(bf16[16,1024,64]{1,2,0:T(8,128)(2,1)S(1)} %bitcast.89) | data formatting | bytes 4194304 | tf_op jit(solution)/shard_map/transpose | solution.py:185
  21.8 4.7 %reshape.108.refs_0_ = bf16[16,65536]{1,0:T(8,128)(2,1)S(1)} reshape(bf16[16,1024,64]{2,1,0:T(8,128)(2,1)} %copy.104) | data formatting | bytes 4194304 | tf_op jit(solution)/shard_map/reshape | solution.py:185
  31.1 2.4 %collective-permute-start.2 = (bf16[6,16,2560]{2,1,0:T(8,128)(2,1)}, bf16[6,16,2560]{2,1,0:T(8,128)(2,1)S(1)}, u32[]{:S(2)}, u32[]{:S(2)}) collective-permute-start(bf16[6,16,2560]{2,1,0:T(8,128)(2,1)} %get-tuple-element.11), channel_id=1, source_target_pairs={{0,4},{4,8},{8,12},{12,16},{16,20},{20,24},{24,28},{1,5},{5,9},{9,... | collective-permute-start | bytes 1474568 | tf_op jit(solution)/shard_map/ppermute | solution.py:179
  33.5 3.9 %collective-permute-start.3 = (bf16[6,16,2560]{2,1,0:T(8,128)(2,1)}, bf16[6,16,2560]{2,1,0:T(8,128)(2,1)S(1)}, u32[]{:S(2)}, u32[]{:S(2)}) collective-permute-start(bf16[6,16,2560]{2,1,0:T(8,128)(2,1)} %get-tuple-element.12), channel_id=1, source_target_pairs={{4,0},{8,4},{12,8},{16,12},{20,16},{24,20},{28,24},{5,1},{9,5},{13... | collective-permute-start | bytes 1474568 | tf_op jit(solution)/shard_map/ppermute | solution.py:179
  37.9 15.7 %collective-permute-done.2 = bf16[6,16,2560]{2,1,0:T(8,128)(2,1)S(1)} collective-permute-done((bf16[6,16,2560]{2,1,0:T(8,128)(2,1)}, bf16[6,16,2560]{2,1,0:T(8,128)(2,1)S(1)}, u32[]{:S(2)}, u32[]{:S(2)}) %collective-permute-start.2) | collective-permute-done | bytes 491552 | tf_op jit(solution)/shard_map/ppermute | solution.py:179
  53.6 4.3 %collective-permute-done.3 = bf16[6,16,2560]{2,1,0:T(8,128)(2,1)S(1)} collective-permute-done((bf16[6,16,2560]{2,1,0:T(8,128)(2,1)}, bf16[6,16,2560]{2,1,0:T(8,128)(2,1)S(1)}, u32[]{:S(2)}, u32[]{:S(2)}) %collective-permute-start.3) | collective-permute-done | bytes 491552 | tf_op jit(solution)/shard_map/ppermute | solution.py:179
  60.0 1.9 %collective-permute-start.4 = (bf16[6,16,2560]{2,1,0:T(8,128)(2,1)S(1)}, bf16[6,16,2560]{2,1,0:T(8,128)(2,1)S(1)}, u32[]{:S(2)}, u32[]{:S(2)}) collective-permute-start(bf16[6,16,2560]{2,1,0:T(8,128)(2,1)S(1)} %copy-done.7), channel_id=1, source_target_pairs={{0,4},{4,8},{8,12},{12,16},{16,20},{20,24},{24,28},{1,5},{5,9},{9,... | collective-permute-start | bytes 1474568 | tf_op jit(solution)/shard_map/ppermute | solution.py:179
  61.9 4.4 %collective-permute-start.5 = (bf16[6,16,2560]{2,1,0:T(8,128)(2,1)S(1)}, bf16[6,16,2560]{2,1,0:T(8,128)(2,1)S(1)}, u32[]{:S(2)}, u32[]{:S(2)}) collective-permute-start(bf16[6,16,2560]{2,1,0:T(8,128)(2,1)S(1)} %copy-done.5), channel_id=1, source_target_pairs={{4,0},{8,4},{12,8},{16,12},{20,16},{24,20},{28,24},{5,1},{9,5},{13... | collective-permute-start | bytes 1474568 | tf_op jit(solution)/shard_map/ppermute | solution.py:179
  66.8 16.1 %collective-permute-done.4 = bf16[6,16,2560]{2,1,0:T(8,128)(2,1)S(1)} collective-permute-done((bf16[6,16,2560]{2,1,0:T(8,128)(2,1)S(1)}, bf16[6,16,2560]{2,1,0:T(8,128)(2,1)S(1)}, u32[]{:S(2)}, u32[]{:S(2)}) %collective-permute-start.4) | collective-permute-done | bytes 491552 | tf_op jit(solution)/shard_map/ppermute | solution.py:179
  82.8 3.6 %collective-permute-done.5 = bf16[6,16,2560]{2,1,0:T(8,128)(2,1)S(1)} collective-permute-done((bf16[6,16,2560]{2,1,0:T(8,128)(2,1)S(1)}, bf16[6,16,2560]{2,1,0:T(8,128)(2,1)S(1)}, u32[]{:S(2)}, u32[]{:S(2)}) %collective-permute-start.5) | collective-permute-done | bytes 491552 | tf_op jit(solution)/shard_map/ppermute | solution.py:179
  95.0 1.8 %copy.120 = f32[1,4,64,1024]{2,3,1,0:T(8,128)S(1)} copy(f32[1,4,64,1024]{3,2,1,0:T(8,128)} %param.14) | data formatting | bytes 2097152 | tf_op args[1]
  99.8 16.0 %shard_map.128 = f32[6,4,2048]{2,1,0:T(4,128)S(1)} custom-call(bf16[4,6,16,2048]{3,2,1,0:T(8,128)(2,1)S(1)} %bitcast.85, bf16[6,16,512]{2,1,0:T(8,128)(2,1)S(1)} %slice.19.latent_ref, bf16[192,48]{1,0:T(8,128)(2,1)S(1)} %copy.113.in_ref, bf16[192,192]{1,0:T(8,128)(2,1)S(1)} %reshape.113.one_ref, bf16[192,192]{1,0:T(8,128)(2,1)S(1)} %reshape.115.two_ref, ...), custom_call_target="tpu_custom_call" | custom-call | flops 2151677952 | bytes 1572864 | tf_op jit(solution)/shard_map/pallas_call | solution.py:127
  117.4 16.0 %shard_map.129 = f32[6,4,2048]{2,1,0:T(4,128)S(1)} custom-call(bf16[4,6,16,2048]{3,2,1,0:T(8,128)(2,1)S(1)} %bitcast.86, bf16[6,16,512]{2,1,0:T(8,128)(2,1)S(1)} %slice.21.latent_ref, bf16[192,48]{1,0:T(8,128)(2,1)S(1)} %copy.113.in_ref, bf16[192,192]{1,0:T(8,128)(2,1)S(1)} %reshape.113.one_ref, bf16[192,192]{1,0:T(8,128)(2,1)S(1)} %reshape.115.two_ref, ...), custom_call_target="tpu_custom_call" | custom-call | flops 2151677952 | bytes 1572864 | tf_op jit(solution)/shard_map/pallas_call | solution.py:127
  133.6 1.9 %collective-permute-start.6 = (bf16[12,4,2048]{2,1,0:T(4,128)(2,1)S(1)}, bf16[12,4,2048]{2,1,0:T(4,128)(2,1)S(1)}, u32[]{:S(2)}, u32[]{:S(2)}) collective-permute-start(bf16[12,4,2048]{2,1,0:T(4,128)(2,1)S(1)} %pad_maximum_fusion.1), channel_id=1, source_target_pairs={{0,4},{4,8},{8,12},{12,16},{16,20},{20,24},{24,28},{1,5},{5,9},{9,... | collective-permute-start | bytes 589832 | tf_op jit(solution)/shard_map/ppermute | solution.py:179
  135.5 4.5 %collective-permute-start.7 = (bf16[12,4,2048]{2,1,0:T(4,128)(2,1)S(1)}, bf16[12,4,2048]{2,1,0:T(4,128)(2,1)S(1)}, u32[]{:S(2)}, u32[]{:S(2)}) collective-permute-start(bf16[12,4,2048]{2,1,0:T(4,128)(2,1)S(1)} %pad_maximum_fusion.1), channel_id=1, source_target_pairs={{4,0},{8,4},{12,8},{16,12},{20,16},{24,20},{28,24},{5,1},{9,5},{13... | collective-permute-start | bytes 589832 | tf_op jit(solution)/shard_map/ppermute | solution.py:179
  140.0 2.3 %collective-permute-done.6 = bf16[12,4,2048]{2,1,0:T(4,128)(2,1)S(1)} collective-permute-done((bf16[12,4,2048]{2,1,0:T(4,128)(2,1)S(1)}, bf16[12,4,2048]{2,1,0:T(4,128)(2,1)S(1)}, u32[]{:S(2)}, u32[]{:S(2)}) %collective-permute-start.6) | collective-permute-done | bytes 196640 | tf_op jit(solution)/shard_map/ppermute | solution.py:179
  142.3 5.1 %collective-permute-done.7 = bf16[12,4,2048]{2,1,0:T(4,128)(2,1)S(1)} collective-permute-done((bf16[12,4,2048]{2,1,0:T(4,128)(2,1)S(1)}, bf16[12,4,2048]{2,1,0:T(4,128)(2,1)S(1)}, u32[]{:S(2)}, u32[]{:S(2)}) %collective-permute-start.7) | collective-permute-done | bytes 196640 | tf_op jit(solution)/shard_map/ppermute | solution.py:179
  149.6 2.2 %reshape.119 = f32[32,4,32,64]{3,2,1,0:T(8,128)} reshape(f32[32,8192]{1,0:T(8,128)S(1)} %convolution_divide_fusion) | data formatting | bytes 2097152 | tf_op jit(solution)/shard_map/reshape | solution.py:293
  151.8 2.0 %copy.119 = f32[32,4,32,64]{3,2,0,1:T(8,128)S(1)} copy(f32[32,4,32,64]{3,2,1,0:T(8,128)} %reshape.119) | data formatting | bytes 2097152 | tf_op jit(solution)/shard_map/reshape | solution.py:293
  154.1 1.9 %fusion = f32[1,4,64,1024]{2,3,1,0:T(8,128)} fusion(f32[1,4,64,1024]{2,3,1,0:T(8,128)S(1)} %copy-done.9, f32[1,4,64,1024]{2,3,1,0:T(8,128)S(1)} %copy.120, f32[4,64,1024]{1,2,0:T(8,128)S(1)} %bitcast.87, f32[]{:T(128)S(6)} %sqrt.19, f32[]{:T(128)S(6)} %sqrt.18, f32[]{:T(128)S(6)} %sqrt.17, f32[]{:T(128)S(6)} %sqrt.16, f32[]{:T(128)S(6)} %sqrt.15), kind=kLoop, calls=%fused_computation.2 | loop fusion | flops 2097152 | bytes 4194324 | tf_op jit(solution)/shard_map/broadcast_in_dim | solution.py:298
  156.0 3.1 %copy.121 = f32[1,4,64,1024]{3,2,1,0:T(8,128)} copy(f32[1,4,64,1024]{2,3,1,0:T(8,128)} %fusion) | data formatting | bytes 2097152 | tf_op jit(solution)/shard_map/broadcast_in_dim | solution.py:298
  (120 shorter events, 22.2 us)
Async XLA Ops:
  6.5 86.6 %copy-start = (bf16[64,64]{1,0:T(8,128)(2,1)S(1)}, bf16[64,64]{1,0:T(8,128)(2,1)}, u32[]{:S(2)}) copy-start(bf16[64,64]{1,0:T(8,128)(2,1)} %param.18) | copy-start | bytes 24580
  6.5 91.9 %all-gather.5.cloned.1.call-start = ((), (), s32[]{:S(2)}) async-start(), calls=%async_computation | async-start | bytes 1966080 | tf_op jit(solution)/shard_map/all_gather | solution.py:253
  7.2 19.3 %collective-permute-start = (s32[6]{0:T(128)S(1)}, s32[6]{0:T(128)S(1)}, u32[]{:S(2)}, u32[]{:S(2)}) collective-permute-start(s32[6]{0:T(128)S(1)} %get-tuple-element.31), channel_id=1, source_target_pairs={{0,4},{4,8},{8,12},{12,16},{16,20},{20,24},{24,28},{1,5},{5,9},{9,... | collective-permute-start | bytes 80 | tf_op jit(solution)/shard_map/ppermute | solution.py:179
  10.4 16.4 %collective-permute-start.1 = (s32[6]{0:T(128)S(1)}, s32[6]{0:T(128)S(1)}, u32[]{:S(2)}, u32[]{:S(2)}) collective-permute-start(s32[6]{0:T(128)S(1)} %get-tuple-element.31), channel_id=1, source_target_pairs={{4,0},{8,4},{12,8},{16,12},{20,16},{24,20},{28,24},{5,1},{9,5},{13... | collective-permute-start | bytes 80 | tf_op jit(solution)/shard_map/ppermute | solution.py:179
  17.0 1.7 %copy-start.10 = (bf16[16,64,1024]{2,1,0:T(8,128)(2,1)S(1)}, bf16[16,64,1024]{2,1,0:T(8,128)(2,1)}, u32[]{:S(2)}) copy-start(bf16[16,64,1024]{2,1,0:T(8,128)(2,1)} %param.15) | copy-start | bytes 6291460
  31.1 28.9 %copy-start.7 = (bf16[6,16,2560]{2,1,0:T(8,128)(2,1)S(1)}, bf16[6,16,2560]{2,1,0:T(8,128)(2,1)}, u32[]{:S(2)}) copy-start(bf16[6,16,2560]{2,1,0:T(8,128)(2,1)} %copy-done.6) | copy-start | bytes 1474564
  31.1 30.8 %copy-start.5 = (bf16[6,16,2560]{2,1,0:T(8,128)(2,1)S(1)}, bf16[6,16,2560]{2,1,0:T(8,128)(2,1)}, u32[]{:S(2)}) copy-start(bf16[6,16,2560]{2,1,0:T(8,128)(2,1)} %copy-done.4) | copy-start | bytes 1474564
  31.1 22.5 %collective-permute-start.2 = (bf16[6,16,2560]{2,1,0:T(8,128)(2,1)}, bf16[6,16,2560]{2,1,0:T(8,128)(2,1)S(1)}, u32[]{:S(2)}, u32[]{:S(2)}) collective-permute-start(bf16[6,16,2560]{2,1,0:T(8,128)(2,1)} %get-tuple-element.11), channel_id=1, source_target_pairs={{0,4},{4,8},{8,12},{12,16},{16,20},{20,24},{24,28},{1,5},{5,9},{9,... | collective-permute-start | bytes 1474568 | tf_op jit(solution)/shard_map/ppermute | solution.py:179
  33.5 24.4 %collective-permute-start.3 = (bf16[6,16,2560]{2,1,0:T(8,128)(2,1)}, bf16[6,16,2560]{2,1,0:T(8,128)(2,1)S(1)}, u32[]{:S(2)}, u32[]{:S(2)}) collective-permute-start(bf16[6,16,2560]{2,1,0:T(8,128)(2,1)} %get-tuple-element.12), channel_id=1, source_target_pairs={{4,0},{8,4},{12,8},{16,12},{20,16},{24,20},{28,24},{5,1},{9,5},{13... | collective-permute-start | bytes 1474568 | tf_op jit(solution)/shard_map/ppermute | solution.py:179
  59.1 34.3 %copy-start.16 = (f32[64]{0:T(128)S(1)}, f32[64]{0:T(128)}, u32[]{:S(2)}) copy-start(f32[64]{0:T(128)} %param.23) | copy-start | bytes 772
  59.1 34.2 %copy-start.17 = (f32[64]{0:T(128)S(1)}, f32[64]{0:T(128)}, u32[]{:S(2)}) copy-start(f32[64]{0:T(128)} %param.24) | copy-start | bytes 772
  59.1 34.2 %copy-start.18 = (f32[64]{0:T(128)S(1)}, f32[64]{0:T(128)}, u32[]{:S(2)}) copy-start(f32[64]{0:T(128)} %param.25) | copy-start | bytes 772
  59.1 34.4 %copy-start.12 = (bf16[64,576]{1,0:T(8,128)(2,1)S(1)}, bf16[64,576]{1,0:T(8,128)(2,1)}, u32[]{:S(2)}) copy-start(bf16[64,576]{1,0:T(8,128)(2,1)} %param.20) | copy-start | bytes 221188
  59.9 34.0 %copy-start.13 = (bf16[64,576]{1,0:T(8,128)(2,1)S(1)}, bf16[64,576]{1,0:T(8,128)(2,1)}, u32[]{:S(2)}) copy-start(bf16[64,576]{1,0:T(8,128)(2,1)} %param.21) | copy-start | bytes 221188
  59.9 56.0 %all-gather.7.cloned.1.call-start = ((), (), s32[]{:S(2)}) async-start(), calls=%async_computation.1 | async-start | bytes 1966080 | tf_op jit(solution)/shard_map/all_gather | solution.py:253
  60.0 22.9 %collective-permute-start.4 = (bf16[6,16,2560]{2,1,0:T(8,128)(2,1)S(1)}, bf16[6,16,2560]{2,1,0:T(8,128)(2,1)S(1)}, u32[]{:S(2)}, u32[]{:S(2)}) collective-permute-start(bf16[6,16,2560]{2,1,0:T(8,128)(2,1)S(1)} %copy-done.7), channel_id=1, source_target_pairs={{0,4},{4,8},{8,12},{12,16},{16,20},{20,24},{24,28},{1,5},{5,9},{9,... | collective-permute-start | bytes 1474568 | tf_op jit(solution)/shard_map/ppermute | solution.py:179
  61.9 24.5 %collective-permute-start.5 = (bf16[6,16,2560]{2,1,0:T(8,128)(2,1)S(1)}, bf16[6,16,2560]{2,1,0:T(8,128)(2,1)S(1)}, u32[]{:S(2)}, u32[]{:S(2)}) collective-permute-start(bf16[6,16,2560]{2,1,0:T(8,128)(2,1)S(1)} %copy-done.5), channel_id=1, source_target_pairs={{4,0},{8,4},{12,8},{16,12},{20,16},{24,20},{28,24},{5,1},{9,5},{13... | collective-permute-start | bytes 1474568 | tf_op jit(solution)/shard_map/ppermute | solution.py:179
  86.5 8.0 %copy-start.14 = (bf16[64,36]{0,1:T(8,128)(2,1)S(1)}, bf16[64,36]{0,1:T(8,128)(2,1)}, u32[]{:S(2)}) copy-start(bf16[64,36]{0,1:T(8,128)(2,1)} %param.19) | copy-start | bytes 13828
  86.6 8.3 %copy-start.11 = (bf16[6,16,2560]{2,1,0:T(8,128)(2,1)}, bf16[6,16,2560]{2,1,0:T(8,128)(2,1)S(1)}, u32[]{:S(2)}) copy-start(bf16[6,16,2560]{2,1,0:T(8,128)(2,1)S(1)} %select_select_fusion) | copy-start | bytes 1474564
  86.6 8.1 %copy-start.15 = (bf16[4,576]{1,0:T(4,128)(2,1)S(1)}, bf16[4,576]{1,0:T(4,128)(2,1)}, u32[]{:S(2)}) copy-start(bf16[4,576]{1,0:T(4,128)(2,1)} %param.22) | copy-start | bytes 13828
  94.1 2.9 %copy-start.19 = (s32[6]{0:T(128)S(1)}, s32[6]{0:T(128)}, u32[]{:S(2)}) copy-start(s32[6]{0:T(128)} %param.16) | copy-start | bytes 76
  133.6 8.7 %collective-permute-start.6 = (bf16[12,4,2048]{2,1,0:T(4,128)(2,1)S(1)}, bf16[12,4,2048]{2,1,0:T(4,128)(2,1)S(1)}, u32[]{:S(2)}, u32[]{:S(2)}) collective-permute-start(bf16[12,4,2048]{2,1,0:T(4,128)(2,1)S(1)} %pad_maximum_fusion.1), channel_id=1, source_target_pairs={{0,4},{4,8},{8,12},{12,16},{16,20},{20,24},{24,28},{1,5},{5,9},{9,... | collective-permute-start | bytes 589832 | tf_op jit(solution)/shard_map/ppermute | solution.py:179
  135.5 11.9 %collective-permute-start.7 = (bf16[12,4,2048]{2,1,0:T(4,128)(2,1)S(1)}, bf16[12,4,2048]{2,1,0:T(4,128)(2,1)S(1)}, u32[]{:S(2)}, u32[]{:S(2)}) collective-permute-start(bf16[12,4,2048]{2,1,0:T(4,128)(2,1)S(1)} %pad_maximum_fusion.1), channel_id=1, source_target_pairs={{4,0},{8,4},{12,8},{16,12},{20,16},{24,20},{28,24},{5,1},{9,5},{13... | collective-permute-start | bytes 589832 | tf_op jit(solution)/shard_map/ppermute | solution.py:179
  151.8 2.2 %copy-start.9 = (f32[1,4,64,1024]{2,3,1,0:T(8,128)S(1)}, f32[1,4,64,1024]{2,3,1,0:T(8,128)}, u32[]{:S(2)}) copy-start(f32[1,4,64,1024]{2,3,1,0:T(8,128)} %copy-done.8) | copy-start | bytes 3145732
  (6 other events, 6.8 us)
Sparse Core Ops, SparseCore 0:
  60.0 19.9 all-gather.4
  87.7 19.9 all-gather.6
